TPU v7x, 256 devices: a whole 4x4x8 slice. The times are simulated.
256 devices in a mesh: dp: 8 (over z), ctx: 32 (over y, x, core).
Axes of the slice: x: 4, y: 4, z: 8, core: 2. Of those that a mesh axis runs over, the one named last changes fastest.
Arguments:
- tokens: bfloat16 [8, 20480, 1024], P('dp', 'ctx'), may hold values from -16 to 16
- slot_keys: bfloat16 [1024, 256], replicated, may hold values from -1 to 1
- w_in: bfloat16 [64, 1024, 4096], P('ctx', None, 'dp'), may hold values from -0.1875 to 0.1875
- w_out: bfloat16 [64, 4096, 1024], P('ctx', 'dp'), may hold values from -0.09375 to 0.09375
- out_grad: bfloat16 [8, 20480, 1024], P('dp', 'ctx'), may hold values from -0.59765625 to 0.59765625
Outputs:
- tokens_grad: bfloat16 [8, 20480, 1024], P('dp', 'ctx')
- slot_keys_grad: float32 [1024, 256], P('ctx')
- w_in_grad: bfloat16 [64, 1024, 4096], P('ctx', None, 'dp')
- w_out_grad: bfloat16 [64, 4096, 1024], P('ctx', 'dp')
All inputs are finite; a program needn't handle non-finite values.
Results may differ from a plain program's by a relative error of at most 0.04.
Values may be sent and summed in bfloat16 or wider, within the bound.
A program may use at most 64 MiB of HBM per device.

v0:
```python
import jax
import jax.numpy as jnp
from jax import lax
from jax.sharding import PartitionSpec as P

S = 4


GELU_A = 0.7978845608028654
GELU_B = 0.044715


def gelu_value(value):
    return 0.5 * value * (1.0 + jnp.tanh(GELU_A * (value + GELU_B * value * value * value)))


def gelu_slope(value):
    inner = jnp.tanh(GELU_A * (value + GELU_B * value * value * value))
    return 0.5 * (1.0 + inner) + 0.5 * value * (1.0 - inner * inner) * GELU_A * (
        1.0 + 3.0 * GELU_B * value * value
    )


def contract_rows(left, right):
    return lax.dot_general(
        left, right, (((0,), (0,)), ((), ())), preferred_element_type=jnp.float32
    )


def contract_cols(left, right):
    return lax.dot_general(
        left, right, (((1,), (1,)), ((), ())), preferred_element_type=jnp.float32
    )


def to_experts(stacked, clip_count, local_experts):
    feature_width = stacked.shape[-1]
    return (
        stacked.reshape(clip_count, local_experts, S, feature_width)
        .transpose(1, 0, 2, 3)
        .reshape(local_experts, clip_count * S, feature_width)
    )


def from_experts(grouped, clip_count, local_experts):
    feature_width = grouped.shape[-1]
    return (
        grouped.reshape(local_experts, clip_count, S, feature_width)
        .transpose(1, 0, 2, 3)
        .reshape(clip_count * local_experts * S, feature_width)
    )


def per_device(tokens, slot_keys, w_in, w_out, out_grad):
    x_local = tokens[0]
    grad_local = out_grad[0]
    clip_count = lax.axis_size("dp")
    local_experts = w_in.shape[0]
    logits = jnp.dot(x_local, slot_keys, preferred_element_type=jnp.float32)
    col_top = lax.pmax(jnp.max(logits, axis=0), "ctx")
    shifted = jnp.exp(logits - col_top[None, :])
    col_total = lax.psum(jnp.sum(shifted, axis=0), "ctx")
    disp_prob = shifted / col_total[None, :]
    comb_prob = jax.nn.softmax(logits, axis=1)
    disp_half = disp_prob.astype(jnp.bfloat16)
    comb_half = comb_prob.astype(jnp.bfloat16)
    slot_own = lax.psum_scatter(
        contract_rows(disp_half, x_local).astype(jnp.bfloat16),
        "ctx",
        scatter_dimension=0,
        tiled=True,
    )
    slot_rows = to_experts(
        lax.all_gather(slot_own, "dp", axis=0, tiled=True), clip_count, local_experts
    )
    pre_act = jnp.einsum("erd,edh->erh", slot_rows, w_in, preferred_element_type=jnp.float32)
    activated = gelu_value(pre_act).astype(jnp.bfloat16)
    out_part = from_experts(
        jnp.einsum("erh,ehd->erd", activated, w_out, preferred_element_type=jnp.float32),
        clip_count,
        local_experts,
    )
    slot_out_own = lax.psum_scatter(
        out_part.astype(jnp.bfloat16), "dp", scatter_dimension=0, tiled=True
    )
    slot_out_all = lax.all_gather(slot_out_own, "ctx", axis=0, tiled=True)
    grad_own = lax.psum_scatter(
        contract_rows(comb_half, grad_local).astype(jnp.bfloat16),
        "ctx",
        scatter_dimension=0,
        tiled=True,
    )
    grad_rows = to_experts(
        lax.all_gather(grad_own, "dp", axis=0, tiled=True), clip_count, local_experts
    )
    act_grad = jnp.einsum("erd,ehd->erh", grad_rows, w_out, preferred_element_type=jnp.float32)
    pre_grad = (act_grad * gelu_slope(pre_act)).astype(jnp.bfloat16)
    w_out_grad = jnp.einsum(
        "erh,erd->ehd", activated, grad_rows, preferred_element_type=jnp.float32
    ).astype(jnp.bfloat16)
    w_in_grad = jnp.einsum(
        "erd,erh->edh", slot_rows, pre_grad, preferred_element_type=jnp.float32
    ).astype(jnp.bfloat16)
    back_part = from_experts(
        jnp.einsum("erh,edh->erd", pre_grad, w_in, preferred_element_type=jnp.float32),
        clip_count,
        local_experts,
    )
    slot_grad_own = lax.psum_scatter(
        back_part.astype(jnp.bfloat16), "dp", scatter_dimension=0, tiled=True
    )
    slot_grad_all = lax.all_gather(slot_grad_own, "ctx", axis=0, tiled=True)
    comb_back = contract_cols(grad_local, slot_out_all)
    disp_back = contract_cols(x_local, slot_grad_all)
    col_inner = lax.psum(jnp.sum(disp_prob * disp_back, axis=0), "ctx")
    disp_part = disp_prob * (disp_back - col_inner[None, :])
    comb_part = comb_prob * (comb_back - jnp.sum(comb_prob * comb_back, axis=1, keepdims=True))
    logit_grad = (disp_part + comb_part).astype(jnp.bfloat16)
    token_grad = contract_cols(logit_grad, slot_keys) + jnp.dot(
        disp_half, slot_grad_all, preferred_element_type=jnp.float32
    )
    key_part = lax.psum_scatter(
        contract_rows(x_local, logit_grad).astype(jnp.bfloat16),
        "ctx",
        scatter_dimension=0,
        tiled=True,
    )
    key_grad = lax.psum(key_part, "dp").astype(jnp.float32)
    return (token_grad.astype(jnp.bfloat16)[None], key_grad, w_in_grad, w_out_grad)


def solution(mesh):
    return jax.shard_map(
        per_device,
        mesh=mesh,
        in_specs=(
            P("dp", "ctx", None),
            P(),
            P("ctx", None, "dp"),
            P("ctx", "dp", None),
            P("dp", "ctx", None),
        ),
        out_specs=(
            P("dp", "ctx", None),
            P("ctx", None),
            P("ctx", None, "dp"),
            P("ctx", "dp", None),
        ),
        check_vma=False,
    )
```

profile of v0, /device:TPU:2, one launch (start us, length us, event | category | flops | bytes accessed | tf_op | source)
XLA Modules:
  0.0 636.2 jit_solution(788827681453766587)
XLA Ops:
  7.2 2.2 fusion.47
  9.4 62.3 %pmax.7 = f32[256]{0:T(256)S(1)} all-reduce(f32[256]{0:T(256)S(1)} %get-tuple-element.21), channel_id=1, replica_groups=mesh['dp'=8,'ctx'=32] {'ctx'}, use_global_device_ids=true, to_apply=%region_1.0 | all-reduce | flops 256 | bytes 2048 | tf_op jit(solution)/shard_map/pmax | solution.py:60
  71.9 62.7 %psum.21 = f32[256]{0:T(256)S(1)} all-reduce(f32[256]{0:T(256)S(1)} %get-tuple-element.19), channel_id=1, replica_groups=mesh['dp'=8,'ctx'=32] {'ctx'}, use_global_device_ids=true, to_apply=%region_3.0 | all-reduce | flops 256 | bytes 2048 | tf_op jit(solution)/shard_map/psum | solution.py:62
  134.6 2.7 fusion.13
  137.4 2.9 fusion.19
  140.4 84.3 %reduce-scatter.10.cloned.1.call-done = bf16[8,1024]{1,0:T(8,128)(2,1)} async-done(((bf16[256,1024]{1,0:T(8,128)(2,1)}), bf16[8,1024]{1,0:T(8,128)(2,1)}) %reduce-scatter.10.cloned.1.call-update) | async-done | bytes 16400 | tf_op jit(solution)/shard_map/reduce_scatter | solution.py:67
  224.7 26.2 %all_gather.13 = bf16[64,1024]{1,0:T(8,128)(2,1)S(1)} all-gather(bf16[8,1024]{1,0:T(8,128)(2,1)} %reduce-scatter.10.cloned.1.call-done), channel_id=1, replica_groups=mesh['dp'=8,'ctx'=32] {'dp'}, dimensions={0}, use_global_device_ids=true | all-gather | bytes 147456 | tf_op jit(solution)/shard_map/all_gather | solution.py:74
  251.1 62.0 %reduce-scatter.8.cloned.1.call-done = bf16[8,1024]{1,0:T(8,128)(2,1)} async-done(((bf16[256,1024]{1,0:T(8,128)(2,1)}), bf16[8,1024]{1,0:T(8,128)(2,1)}) %reduce-scatter.8.cloned.1.call-update) | async-done | bytes 16400 | tf_op jit(solution)/shard_map/reduce_scatter | solution.py:87
  313.1 26.2 %all_gather.12 = bf16[64,1024]{1,0:T(8,128)(2,1)S(1)} all-gather(bf16[8,1024]{1,0:T(8,128)(2,1)} %reduce-scatter.8.cloned.1.call-done), channel_id=1, replica_groups=mesh['dp'=8,'ctx'=32] {'dp'}, dimensions={0}, use_global_device_ids=true | all-gather | bytes 147456 | tf_op jit(solution)/shard_map/all_gather | solution.py:94
  339.4 2.0 fusion.48
  341.9 0.7 fusion.31
  343.1 0.7 convolution_convert_fusion.3
  343.8 0.7 convert_element_type.69
  344.5 0.9 copy.35
  345.5 0.7 convert_element_type.71
  347.0 2.1 convolution_convert_fusion
  349.2 32.8 %reduce-scatter.14.cloned.1.call-done = bf16[8,1024]{1,0:T(8,128)(2,1)} async-done(((bf16[64,1024]{1,0:T(8,128)(2,1)}), bf16[8,1024]{1,0:T(8,128)(2,1)}) %reduce-scatter.14.cloned.1.call-update) | async-done | bytes 16400 | tf_op jit(solution)/shard_map/reduce_scatter | solution.py:83
  382.0 24.4 %all_gather.15 = bf16[256,1024]{1,0:T(8,128)(2,1)S(1)} all-gather(bf16[8,1024]{1,0:T(8,128)(2,1)} %reduce-scatter.14.cloned.1.call-done), channel_id=1, replica_groups=mesh['dp'=8,'ctx'=32] {'ctx'}, dimensions={0}, use_global_device_ids=true | all-gather | bytes 540672 | tf_op jit(solution)/shard_map/all_gather | solution.py:86
  406.5 1.9 fusion.25
  408.3 11.9 %reduce-scatter.12.cloned.1.call-done = bf16[8,1024]{1,0:T(8,128)(2,1)} async-done(((bf16[64,1024]{1,0:T(8,128)(2,1)}), bf16[8,1024]{1,0:T(8,128)(2,1)}) %reduce-scatter.12.cloned.1.call-update) | async-done | bytes 16400 | tf_op jit(solution)/shard_map/reduce_scatter | solution.py:109
  420.2 24.5 %all_gather.14 = bf16[256,1024]{1,0:T(8,128)(2,1)S(1)} all-gather(bf16[8,1024]{1,0:T(8,128)(2,1)} %reduce-scatter.12.cloned.1.call-done), channel_id=1, replica_groups=mesh['dp'=8,'ctx'=32] {'ctx'}, dimensions={0}, use_global_device_ids=true | all-gather | bytes 540672 | tf_op jit(solution)/shard_map/all_gather | solution.py:112
  444.7 3.5 multiply_reduce_fusion.1
  448.2 60.7 %psum.22 = f32[256]{0:T(256)S(1)} all-reduce(f32[256]{0:T(256)} %get-tuple-element.16), channel_id=1, replica_groups=mesh['dp'=8,'ctx'=32] {'ctx'}, use_global_device_ids=true, to_apply=%region_10.0 | all-reduce | flops 256 | bytes 2048 | tf_op jit(solution)/shard_map/psum | solution.py:115
  508.9 1.7 add_convert_fusion.1
  510.6 1.4 fusion.28
  512.0 2.1 copy.30
  514.1 2.1 convolution_convert_fusion.1
  517.2 1.6 fusion
  518.8 78.6 %reduce-scatter.16.cloned.1.call-done = bf16[32,256]{1,0:T(8,128)(2,1)} async-done(((bf16[1024,256]{1,0:T(8,128)(2,1)}), bf16[32,256]{1,0:T(8,128)(2,1)}) %reduce-scatter.16.cloned.1.call-update) | async-done | bytes 16400
  597.4 0.8 copy.31
  598.3 30.7 %psum.23 = bf16[32,256]{0,1:T(8,128)(2,1)S(1)} all-reduce(bf16[32,256]{0,1:T(8,128)(2,1)S(1)} %copy.31), channel_id=1, replica_groups=mesh['dp'=8,'ctx'=32] {'dp'}, use_global_device_ids=true, to_apply=%region_14.0 | all-reduce | flops 8192 | bytes 32768 | tf_op jit(solution)/shard_map/psum | solution.py:128
  629.0 0.7 copy.27
  (40 shorter events, 3.6 us)
Async XLA Ops:
  7.2 334.3 %copy-start = (bf16[2,512,1024]{2,1,0:T(8,128)(2,1)S(1)}, bf16[2,512,1024]{2,1,0:T(8,128)(2,1)}, u32[]{:S(2)}) copy-start(bf16[2,512,1024]{2,1,0:T(8,128)(2,1)} %param.8) | copy-start | bytes 6291460
  7.2 217.6 %reduce-scatter.10.cloned.1.call-start = ((), (), s32[]{:S(2)}) async-start(), calls=%async_computation.6 | async-start | bytes 540672 | tf_op jit(solution)/shard_map/reduce_scatter | solution.py:67
  137.4 175.7 %reduce-scatter.8.cloned.1.call-start = ((), (), s32[]{:S(2)}) async-start(), calls=%async_computation.5 | async-start | bytes 540672 | tf_op jit(solution)/shard_map/reduce_scatter | solution.py:87
  140.4 241.7 %reduce-scatter.14.cloned.1.call-start = ((), (), s32[]{:S(2)}) async-start(), calls=%async_computation.8 | async-start | bytes 147456 | tf_op jit(solution)/shard_map/reduce_scatter | solution.py:83
  341.5 1.6 copy-start.1
  343.1 6.0 copy-start.6
  347.0 73.2 %reduce-scatter.12.cloned.1.call-start = ((), (), s32[]{:S(2)}) async-start(), calls=%async_computation.7 | async-start | bytes 147456 | tf_op jit(solution)/shard_map/reduce_scatter | solution.py:109
  349.1 248.3 %reduce-scatter.16.cloned.1.call-start = ((), (), s32[]{:S(2)}) async-start(), calls=%async_computation.9 | async-start | bytes 540672
  408.3 39.9 %copy-start.2 = (f32[640,256]{1,0:T(8,128)}, f32[640,256]{1,0:T(8,128)S(1)}, u32[]{:S(2)}) copy-start(f32[640,256]{1,0:T(8,128)S(1)} %fusion.25) | copy-start | bytes 1966084
  444.7 3.5 copy-start.3
  508.8 1.7 copy-start.5
  510.6 3.5 copy-start.7
  514.1 2.1 copy-start.8
  516.2 1.0 copy-start.4
Sparse Core Ops, SparseCore 0:
  137.5 87.2 reduce-scatter.9
  229.0 83.9 reduce-scatter.7
  347.1 34.8 reduce-scatter.13
  385.1 35.0 reduce-scatter.11
  514.2 83.1 reduce-scatter.15
where the time goes:
time: 637 us; the launch traced here: 636 us
  blocking collectives  318 us (50%)
  waiting for transfers between devices  270 us (42%)
  matrix products  24.7 us (4%)
  between operations  13.9 us (2%)
  local copies, waits for them, and re-layouts  7.99 us (1%)
    reduce_scatter x1, waiting for transfers between devices, per_device(): lax.psum_scatter(contract_rows(disp_half, x_local).astype(jnp.bfloat16),...  84.3 us
    unnamed x6, waiting for transfers between devices  78.7 us
    psum x1, blocking collectives, per_device(): col_total = lax.psum(jnp.sum(shifted, axis=0), 'ctx')  62.7 us
    pmax x1, blocking collectives, per_device(): col_top = lax.pmax(jnp.max(logits, axis=0), 'ctx')  62.3 us
    reduce_scatter x1, waiting for transfers between devices, per_device(): lax.psum_scatter(contract_rows(comb_half, grad_local).astype(jnp.bfloat16...  62 us
    psum x1, blocking collectives, per_device(): col_inner = lax.psum(jnp.sum(disp_prob * disp_back, axis=0), 'ctx')  60.7 us
    reduce_scatter x1, waiting for transfers between devices, per_device(): lax.psum_scatter(out_part.astype(jnp.bfloat16), 'dp', scatter_dimension=0...  32.8 us
    psum x1, blocking collectives, per_device(): key_grad = lax.psum(key_part, 'dp').astype(jnp.float32)  30.7 us
  transfers between devices with their start and end apart: 5, of which 5 were waited for; matrix products, arithmetic and copies ran while one was open for 2% of the time, Pallas kernels for 0%

commit v1 on v0

v1 whole, which is shorter than its diff:
```python
import jax
import jax.numpy as jnp
from jax import lax
from jax.experimental import pallas as pl
from jax.experimental.pallas import tpu as pltpu
from jax.sharding import PartitionSpec as P

MESH = pl.DeviceIdType.MESH
BF = jnp.bfloat16
F32 = jnp.float32

T = 640
D = 1024
S = 256
HL = 512
NZ = 8
SIDE = 4
NC = SIDE * SIDE

GELU_A = 0.7978845608028654
GELU_B = 0.044715


def gelu_value(value):
    return 0.5 * value * (1.0 + jnp.tanh(GELU_A * (value + GELU_B * value * value * value)))


def gelu_slope(value):
    inner = jnp.tanh(GELU_A * (value + GELU_B * value * value * value))
    return 0.5 * (1.0 + inner) + 0.5 * value * (1.0 - inner * inner) * GELU_A * (
        1.0 + 3.0 * GELU_B * value * value
    )


def nn(a, b):
    return lax.dot_general(a, b, (((1,), (0,)), ((), ())), preferred_element_type=F32)


def nt(a, b):
    return lax.dot_general(a, b, (((1,), (1,)), ((), ())), preferred_element_type=F32)


def tn(a, b):
    return lax.dot_general(a, b, (((0,), (0,)), ((), ())), preferred_element_type=F32)


def fold(rows):
    return jnp.concatenate([rows[:, : D // 2], rows[:, D // 2 :]], axis=0)


def unfold(rows):
    return jnp.concatenate([rows[:8], rows[8:]], axis=1)


def lanes(shape, columns):
    at = lax.broadcasted_iota(jnp.int32, shape, 1)
    tile = jnp.zeros(shape, F32)
    for i, column in enumerate(columns):
        tile = jnp.where(at == i, column, tile)
    return tile


def split2(value):
    high = value.astype(BF).astype(F32)
    return high, value - high


def kernel(
    x_hbm, keys_hbm, wi_hbm, wo_hbm, g_hbm,
    tg_hbm, kg_hbm, wig_hbm, wog_hbm,
    x, keys, wi, wo, g,
    keysT, LT, comb, combH, disp, xT,
    gs_send, gs_recv, gsum, gpk, garr,
    us_send, us_recv, usum, ustat, upk, uarr,
    rown, zg, zu, gall, rall, pre, act, pg, outp,
    cpk, crecv, bpk, brecv,
    so, si, sof, sif, cpart, lgH, lgN, dispH,
    ks_send, ks_recv, ksum, kpk, karr, kz, kzarr, kout,
    tgs, wigs, wogs,
    ld, st, sib_s, sib_r,
    ag_s, ag_r, au_s, au_r,
    bg_s, bg_r, bu_s, bu_r,
    co_s, co_r, cb_s, cb_r,
    do_s, do_r, db_s, db_r, fo_s, fo_r, fb_s, fb_r,
    fk_s, fk_r, fz_s, fz_r,
):
    dp = lax.axis_index("dp")
    ctx = lax.axis_index("ctx")
    core = lax.rem(ctx, 2)
    chip = lax.div(ctx, 2)
    cy, cx = lax.div(chip, SIDE), lax.rem(chip, SIDE)
    other = 1 - core
    sib = {"ctx": chip * 2 + other}

    def ahead(d):
        return lax.rem(cy + lax.div(d, SIDE), SIDE) * SIDE + lax.rem(cx + lax.rem(d, SIDE), SIDE)

    def behind(d):
        return (
            lax.rem(cy + SIDE - lax.div(d, SIDE), SIDE) * SIDE
            + lax.rem(cx + SIDE - lax.rem(d, SIDE), SIDE)
        )

    def zahead(e):
        return lax.rem(dp + e, NZ)

    def zbehind(e):
        return lax.rem(dp + NZ - e, NZ)

    def loop(lo, hi, body):
        def step(i, carry):
            body(i)
            return carry

        lax.fori_loop(lo, hi, step, 0)

    def remote(src, dst, send, recv, device):
        return pltpu.make_async_remote_copy(
            src_ref=src, dst_ref=dst, send_sem=send, recv_sem=recv,
            device_id=device, device_id_type=MESH,
        )

    load_keys = pltpu.make_async_copy(keys_hbm, keys, ld.at[0])
    load_x = pltpu.make_async_copy(x_hbm, x, ld.at[1])
    load_g = pltpu.make_async_copy(g_hbm, g, ld.at[2])
    load_wo = pltpu.make_async_copy(wo_hbm, wo, ld.at[3])
    load_wi = pltpu.make_async_copy(wi_hbm, wi, ld.at[4])
    for copy in (load_keys, load_x, load_g, load_wo, load_wi):
        copy.start()

    barrier = pltpu.get_barrier_semaphore()
    pl.semaphore_signal(barrier, inc=1, device_id=sib, device_id_type=MESH)

    def greet_plane(d):
        pl.semaphore_signal(
            barrier, inc=1, device_id={"ctx": ahead(d) * 2 + core}, device_id_type=MESH
        )

    loop(1, NC, greet_plane)

    def greet_z(e):
        pl.semaphore_signal(barrier, inc=1, device_id={"dp": zahead(e)}, device_id_type=MESH)

    loop(1, NZ, greet_z)

    load_keys.wait()
    for b in range(D // 128):
        block = keys[b * 128 : (b + 1) * 128, :].astype(F32).T
        keysT[:, b * 128 : (b + 1) * 128] = jnp.concatenate(
            [block[(2 * j + k) * 8 : (2 * j + k) * 8 + 8] for k in range(2) for j in range(NC)], axis=0
        ).astype(BF)
    load_x.wait()
    LT[...] = nt(keysT[...], x[...])
    for t in range(T // 128):
        at = slice(t * 128, (t + 1) * 128)
        logit = LT[:, at]
        e = jnp.exp(logit - jnp.max(logit, axis=0, keepdims=True))
        e = e / jnp.sum(e, axis=0, keepdims=True)
        comb[:, at] = e
        combH[:, at] = e.astype(BF)
    load_g.wait()
    mine = pl.ds(pl.multiple_of(core * 128, 128), 128)
    theirs = pl.ds(pl.multiple_of(other * 128, 128), 128)
    gs_send[...] = nn(combH[theirs, :], g[...]).astype(BF)
    pl.semaphore_wait(barrier, NC + NZ - 1)
    sib_g = remote(gs_send, gs_recv, sib_s.at[0], sib_r.at[0], sib)
    sib_g.start()
    gsum[...] = nn(combH[mine, :], g[...])

    logit = LT[...]
    top = jnp.max(logit, axis=1, keepdims=True).astype(BF).astype(F32)
    e = jnp.exp(logit - top)
    total = jnp.sum(e, axis=1, keepdims=True)
    disp[...] = e.astype(BF)
    high, low = split2(total)
    ustat[...] = lanes((S, 128), (top, high, low))
    us_send[:, :D] = nn(disp[theirs, :], x[...]).astype(BF)
    us_send[:, D:] = ustat[theirs, :].astype(BF)
    sib_u = remote(us_send, us_recv, sib_s.at[1], sib_r.at[1], sib)
    sib_u.start()

    sib_g.wait_recv()
    gsum[...] += gs_recv[...].astype(F32)

    def ag(d):
        j = ahead(d)
        return remote(gpk.at[j], garr.at[d], ag_s.at[d], ag_r.at[d], {"ctx": j * 2 + core})

    def send_g(d):
        j = ahead(d)
        gpk[j] = fold(gsum[pl.ds(pl.multiple_of(j * 8, 8), 8), :]).astype(BF)
        ag(d).start()

    loop(1, NC, send_g)

    usum[...] = nn(disp[mine, :], x[...])
    own = ustat[mine, :]
    sib_u.wait_recv()
    got = us_recv[:, D:].astype(F32)
    top_a, top_b = own[:, 0:1], got[:, 0:1]
    top = jnp.maximum(top_a, top_b)
    wa, wb = jnp.exp(top_a - top), jnp.exp(top_b - top)
    total = (own[:, 1:2] + own[:, 2:3]) * wa + (got[:, 1:2] + got[:, 2:3]) * wb
    usum[...] = usum[...] * wa + us_recv[:, :D].astype(F32) * wb
    high, low = split2(total)
    ustat[0:128, :] = lanes((128, 128), (top, high, low))

    def pack_u(j):
        at = pl.ds(pl.multiple_of(j * 8, 8), 8)
        s = ustat[at, :]
        return jnp.concatenate([fold(usum[at, :]), jnp.concatenate([s, s], axis=0)], axis=1)

    def au(d):
        j = ahead(d)
        return remote(upk.at[j], uarr.at[d], au_s.at[d], au_r.at[d], {"ctx": j * 2 + core})

    def send_u(d):
        j = ahead(d)
        upk[j] = pack_u(j).astype(BF)
        au(d).start()

    loop(1, NC, send_u)

    for b in range(D // 128):
        block = x[:, b * 128 : (b + 1) * 128].astype(F32).T.astype(BF)
        xT[0, b * 64 : (b + 1) * 64, :] = jnp.concatenate([block[0:32], block[64:96]], axis=0)
        xT[1, b * 64 : (b + 1) * 64, :] = jnp.concatenate([block[32:64], block[96:128]], axis=0)

    def add_g(d, acc):
        ag(d).wait_recv()
        return acc + garr[d].astype(F32)

    acc = fold(gsum[pl.ds(pl.multiple_of(chip * 8, 8), 8), :])
    zg[dp] = lax.fori_loop(1, NC, add_g, acc).astype(BF)

    def bg(e):
        return remote(zg.at[dp], zg.at[dp], bg_s.at[e], bg_r.at[e], {"dp": zahead(e)})

    def bg_in(e):
        j = zbehind(e)
        return remote(zg.at[j], zg.at[j], bg_s.at[e], bg_r.at[e], {"dp": zahead(e)})

    loop(1, NZ, lambda e: bg(e).start())

    uarr[0] = pack_u(chip).astype(BF)
    half = D // 2

    def top_u(d, top):
        au(d).wait_recv()
        return jnp.maximum(top, uarr[d, :, half : half + 128].astype(F32))

    tops = lax.fori_loop(1, NC, top_u, uarr[0, :, half : half + 128].astype(F32))
    top = tops[:, 0:1]

    def add_u(d, carry):
        acc, total = carry
        piece = uarr[d].astype(F32)
        w = jnp.exp(piece[:, half : half + 1] - top)
        total = total + w * (piece[:, half + 1 : half + 2] + piece[:, half + 2 : half + 3])
        return acc + w * piece[:, :half], total

    acc, total = lax.fori_loop(
        0, NC, add_u, (jnp.zeros((16, half), F32), jnp.zeros((16, 1), F32))
    )
    acc = acc / total
    rown[...] = acc
    zu[dp] = acc.astype(BF)

    def bu(e):
        return remote(zu.at[dp], zu.at[dp], bu_s.at[e], bu_r.at[e], {"dp": zahead(e)})

    def bu_in(e):
        j = zbehind(e)
        return remote(zu.at[j], zu.at[j], bu_s.at[e], bu_r.at[e], {"dp": zahead(e)})

    loop(1, NZ, lambda e: bu(e).start())

    first = lax.rem(lax.broadcasted_iota(jnp.int32, (64, HL), 0), 8) < 4
    loop(1, NZ, lambda e: bg_in(e).wait_recv())
    gall[...] = jnp.concatenate([unfold(zg[c].astype(F32)) for c in range(NZ)], axis=0).astype(BF)
    load_wo.wait()
    act_grad = jnp.where(first, nt(gall[...], wo[0]), nt(gall[...], wo[1]))
    pre[...] = act_grad
    loop(1, NZ, lambda e: bu_in(e).wait_recv())
    rall[...] = jnp.concatenate([unfold(zu[c].astype(F32)) for c in range(NZ)], axis=0).astype(BF)
    load_wi.wait()
    pre_act = jnp.where(first, nn(rall[...], wi[0]), nn(rall[...], wi[1]))
    a = gelu_value(pre_act)
    act[0] = jnp.where(first, a, 0.0).astype(BF)
    act[1] = jnp.where(first, 0.0, a).astype(BF)
    p = pre[...] * gelu_slope(pre_act)
    pg[0] = jnp.where(first, p, 0.0).astype(BF)
    pg[1] = jnp.where(first, 0.0, p).astype(BF)

    def co(e):
        j = zahead(e)
        return remote(cpk.at[j], crecv.at[e], co_s.at[e], co_r.at[e], {"dp": j})

    def cb(e):
        j = zahead(e)
        return remote(bpk.at[j], brecv.at[e], cb_s.at[e], cb_r.at[e], {"dp": j})

    def clip_rows(j):
        return fold(outp[pl.ds(pl.multiple_of(j * 8, 8), 8), :])

    def send_o(e):
        j = zahead(e)
        cpk[j] = clip_rows(j).astype(BF)
        co(e).start()

    outp[...] = nn(act[0], wo[0]) + nn(act[1], wo[1])
    loop(1, NZ, send_o)
    o_own = clip_rows(dp)

    def send_b(e):
        j = zahead(e)
        bpk[j] = clip_rows(j).astype(BF)
        cb(e).start()

    outp[...] = nt(pg[0], wi[0]) + nt(pg[1], wi[1])
    loop(1, NZ, send_b)
    b_own = clip_rows(dp)

    for e in range(2):
        for c in range(HL // 128):
            at = slice(c * 128, (c + 1) * 128)
            wogs[e, at, :] = tn(act[e, :, at], gall[...]).astype(BF)
    store_wo = pltpu.make_async_copy(wogs, wog_hbm, st.at[0])
    store_wo.start()

    def add_o(e, acc):
        co(e).wait_recv()
        return acc + crecv[e].astype(F32)

    so[core, chip] = lax.fori_loop(1, NZ, add_o, o_own).astype(BF)

    def do(d):
        return remote(
            so.at[core, chip], so.at[core, chip], do_s.at[d], do_r.at[d], {"ctx": ahead(d) * 2 + core}
        )

    def fo(d):
        j = behind(d)
        return remote(so.at[core, j], so.at[core, j], fo_s.at[d], fo_r.at[d], sib)

    loop(1, NC, lambda d: do(d).start())
    fo(0).start()

    def add_b(e, acc):
        cb(e).wait_recv()
        return acc + brecv[e].astype(F32)

    back = lax.fori_loop(1, NZ, add_b, b_own).astype(BF)
    si[core, chip, :, :half] = back
    inner = jnp.sum(rown[...] * back.astype(F32), axis=1, keepdims=True)
    inner = inner[:8] + inner[8:]
    inner = jnp.concatenate([inner, inner], axis=0)
    z_high, z_low = split2(total)
    i_high, i_low = split2(inner)
    si[core, chip, :, half:] = lanes((16, 128), (top, z_high, z_low, i_high, i_low)).astype(BF)

    def db(d):
        return remote(
            si.at[core, chip], si.at[core, chip], db_s.at[d], db_r.at[d], {"ctx": ahead(d) * 2 + core}
        )

    def fb(d):
        j = behind(d)
        return remote(si.at[core, j], si.at[core, j], fb_s.at[d], fb_r.at[d], sib)

    loop(1, NC, lambda d: db(d).start())
    fb(0).start()

    def pass_o(d):
        do(d).wait_recv()
        fo(d).start()

    loop(1, NC, pass_o)

    def pass_b(d):
        db(d).wait_recv()
        fb(d).start()

    for e in range(2):
        for c in range(D // 128):
            at = slice(c * 128, (c + 1) * 128)
            wigs[e, at, :] = tn(rall[:, at], pg[e]).astype(BF)
    store_wi = pltpu.make_async_copy(wigs, wig_hbm, st.at[1])
    store_wi.start()

    loop(1, NC, pass_b)
    loop(0, NC, lambda d: fo(d).wait_recv())

    def rows_of(ref, k, q):
        return jnp.concatenate(
            [unfold(ref[k, 2 * q, :, :half].astype(F32)), unfold(ref[k, 2 * q + 1, :, :half].astype(F32))],
            axis=0,
        ).astype(BF)

    for k in range(2):
        for q in range(NC // 2):
            at = k * 128 + q * 16
            sof[at : at + 16, :] = rows_of(so, k, q)
    cpart[...] = nt(sof[...], g[...])
    for t in range(T // 128):
        at = slice(t * 128, (t + 1) * 128)
        prob, back = comb[:, at], cpart[:, at]
        cpart[:, at] = prob * (back - jnp.sum(prob * back, axis=0, keepdims=True))

    loop(0, NC, lambda d: fb(d).wait_recv())
    for k in range(2):
        for q in range(NC // 2):
            at = k * 128 + q * 16
            sif[at : at + 16, :] = rows_of(si, k, q)
    stat = jnp.concatenate(
        [si[k, j, 0:8, half : half + 128].astype(F32) for k in range(2) for j in range(NC)], axis=0
    )
    top = stat[:, 0:1]
    over = 1.0 / (stat[:, 1:2] + stat[:, 2:3])
    inner = stat[:, 3:4] + stat[:, 4:5]
    comb[...] = nt(sif[...], x[...])
    for t in range(T // 128):
        at = slice(t * 128, (t + 1) * 128)
        prob = jnp.exp(LT[:, at] - top) * over
        dispH[:, at] = prob.astype(BF)
        lg = prob * (comb[:, at] - inner) + cpart[:, at]
        lgH[:, at] = lg.astype(BF)
        lgN[:, at] = jnp.concatenate(
            [lg[k * 128 + j * 8 : k * 128 + j * 8 + 8] for j in range(NC) for k in range(2)], axis=0
        ).astype(BF)

    ks_send[...] = nt(xT[other], lgN[...]).astype(BF)
    sib_k = remote(ks_send, ks_recv, sib_s.at[2], sib_r.at[2], sib)
    sib_k.start()
    ksum[...] = nt(xT[core], lgN[...])
    sib_k.wait_recv()
    ksum[...] += ks_recv[...].astype(F32)

    def fk(d):
        j = ahead(d)
        return remote(kpk.at[j], karr.at[d], fk_s.at[d], fk_r.at[d], {"ctx": j * 2 + core})

    def key_rows(j):
        return ksum[pl.ds(pl.multiple_of(j * 32, 32), 32), :]

    def send_k(d):
        j = ahead(d)
        kpk[j] = key_rows(j).astype(BF)
        fk(d).start()

    loop(1, NC, send_k)

    for t in range(T // 128):
        at = slice(t * 128, (t + 1) * 128)
        tgs[at, :] = (tn(lgH[:, at], keysT[...]) + tn(dispH[:, at], sif[...])).astype(BF)
    store_tg = pltpu.make_async_copy(tgs, tg_hbm, st.at[2])
    store_tg.start()

    def add_k(d, acc):
        fk(d).wait_recv()
        return acc + karr[d].astype(F32)

    acc = lax.fori_loop(1, NC, add_k, key_rows(chip))
    kz[...] = acc.astype(BF)

    def fz(e):
        return remote(kz, kzarr.at[e], fz_s.at[e], fz_r.at[e], {"dp": zahead(e)})

    loop(1, NZ, lambda e: fz(e).start())

    def add_z(e, acc):
        fz(e).wait_recv()
        return acc + kzarr[e].astype(F32)

    kout[...] = lax.fori_loop(1, NZ, add_z, acc)
    store_kg = pltpu.make_async_copy(kout, kg_hbm, st.at[3])
    store_kg.start()

    sib_g.wait_send()
    sib_u.wait_send()
    sib_k.wait_send()

    def drain_plane(d):
        ag(d).wait_send()
        au(d).wait_send()
        do(d).wait_send()
        db(d).wait_send()
        fk(d).wait_send()

    loop(1, NC, drain_plane)

    def drain_pass(d):
        fo(d).wait_send()
        fb(d).wait_send()

    loop(0, NC, drain_pass)

    def drain_z(e):
        bg(e).wait_send()
        bu(e).wait_send()
        co(e).wait_send()
        cb(e).wait_send()
        fz(e).wait_send()

    loop(1, NZ, drain_z)
    store_wo.wait()
    store_wi.wait()
    store_tg.wait()
    store_kg.wait()


def per_device(tokens, slot_keys, w_in, w_out, out_grad):
    hbm = pl.BlockSpec(memory_space=pl.ANY)
    vmem = pltpu.VMEM
    half = D // 2
    plane, line = pltpu.SemaphoreType.DMA((NC,)), pltpu.SemaphoreType.DMA((NZ,))
    tg, kg, wig, wog = pl.pallas_call(
        kernel,
        out_shape=(
            jax.ShapeDtypeStruct((T, D), BF),
            jax.ShapeDtypeStruct((32, S), F32),
            jax.ShapeDtypeStruct((2, D, HL), BF),
            jax.ShapeDtypeStruct((2, HL, D), BF),
        ),
        in_specs=[hbm] * 5,
        out_specs=(hbm,) * 4,
        scratch_shapes=[
            vmem((T, D), BF), vmem((D, S), BF), vmem((2, D, HL), BF), vmem((2, HL, D), BF), vmem((T, D), BF),
            vmem((S, D), BF), vmem((S, T), F32), vmem((S, T), F32), vmem((S, T), BF), vmem((S, T), BF),
            vmem((2, D // 2, T), BF),
            vmem((128, D), BF), vmem((128, D), BF), vmem((128, D), F32),
            vmem((NC, 16, half), BF), vmem((NC, 16, half), BF),
            vmem((128, D + 128), BF), vmem((128, D + 128), BF), vmem((128, D), F32), vmem((S, 128), F32),
            vmem((NC, 16, half + 128), BF), vmem((NC, 16, half + 128), BF),
            vmem((16, half), F32), vmem((NZ, 16, half), BF), vmem((NZ, 16, half), BF),
            vmem((64, D), BF), vmem((64, D), BF), vmem((64, HL), F32),
            vmem((2, 64, HL), BF), vmem((2, 64, HL), BF), vmem((64, D), F32),
            vmem((NZ, 16, half), BF), vmem((NZ, 16, half), BF),
            vmem((NZ, 16, half), BF), vmem((NZ, 16, half), BF),
            vmem((2, NC, 16, half), BF), vmem((2, NC, 16, half + 128), BF), vmem((S, D), BF), vmem((S, D), BF),
            vmem((S, T), F32), vmem((S, T), BF), vmem((S, T), BF), vmem((S, T), BF),
            vmem((D // 2, S), BF), vmem((D // 2, S), BF), vmem((D // 2, S), F32),
            vmem((NC, 32, S), BF), vmem((NC, 32, S), BF), vmem((32, S), BF), vmem((NZ, 32, S), BF),
            vmem((32, S), F32),
            vmem((T, D), BF), vmem((2, D, HL), BF), vmem((2, HL, D), BF),
            pltpu.SemaphoreType.DMA((5,)), pltpu.SemaphoreType.DMA((4,)),
            pltpu.SemaphoreType.DMA((3,)), pltpu.SemaphoreType.DMA((3,)),
            plane, plane, plane, plane,
            line, line, line, line,
            line, line, line, line,
            plane, plane, plane, plane, plane, plane, plane, plane,
            plane, plane, line, line,
        ],
        compiler_params=pltpu.CompilerParams(
            collective_id=0, has_side_effects=True, vmem_limit_bytes=60 * 2**20
        ),
        cost_estimate=pl.CostEstimate(flops=4 * 10**9, bytes_accessed=13 * 10**6, transcendentals=10**6),
    )(tokens[0], slot_keys, w_in, w_out, out_grad[0])
    return tg[None], kg, wig, wog


def solution(mesh):
    return jax.shard_map(
        per_device,
        mesh=mesh,
        in_specs=(
            P("dp", "ctx", None),
            P(),
            P("ctx", None, "dp"),
            P("ctx", "dp", None),
            P("dp", "ctx", None),
        ),
        out_specs=(
            P("dp", "ctx", None),
            P("ctx", None),
            P("ctx", None, "dp"),
            P("ctx", "dp", None),
        ),
        check_vma=False,
    )
```

time: 637 us -> 72.2 us (0.11)
  blocking collectives: 318 us -> 0 us
  waiting for transfers between devices: 270 us -> 0 us
  Pallas kernels: 0 us -> 64.3 us
  matrix products: 24.7 us -> 0 us
  between operations: 13.9 us -> 0.66 us
    reduce_scatter x4 -> x0, waiting for transfers between devices: 191 us -> none  [the longest x1 84.3 us: per_device(): lax.psum_scatter(contract_rows(disp_half, x_local).astype(jnp.bfloat16),...]
    psum x3 -> x0, blocking collectives: 154 us -> none  [the longest x1 62.7 us: per_device(): col_total = lax.psum(jnp.sum(shifted, axis=0), 'ctx')]
    all_gather x4 -> x0, blocking collectives: 101 us -> none  [the longest x1 26.2 us: per_device(): lax.all_gather(grad_own, 'dp', axis=0, tiled=True)]
    unnamed x6 -> x0, waiting for transfers between devices: 78.7 us -> none
    pallas_call x0 -> x1, Pallas kernels: none -> 64.3 us  [per_device(): pl.pallas_call(kernel, out_shape=(jax.ShapeDtypeStruct((T, D), BF), jax.S...]
    pmax x1 -> x0, blocking collectives: 62.3 us -> none  [per_device(): col_top = lax.pmax(jnp.max(logits, axis=0), 'ctx')]
    dot_general x14 -> x0, matrix products: 24.7 us -> none  [the longest x3 7.04 us: contract_rows(): lax.dot_general(left, right, (((0,), (0,)), ((), ())), preferred_element_...]
  transfers between devices with their start and end apart: 5 -> 0, of which waited for: 5 -> 0; matrix products, arithmetic and copies ran while one was open for 2% -> 0% of each run, Pallas kernels for 0% -> 0%
where the time goes in v1:
time: 72.2 us; the launch traced here: 71.9 us
  Pallas kernels  64.3 us (89%)
  local copies, waits for them, and re-layouts  6.9 us (10%)
    pallas_call x1, Pallas kernels, per_device(): pl.pallas_call(kernel, out_shape=(jax.ShapeDtypeStruct((T, D), BF), jax.S...  64.3 us
    unnamed x10, local copies, waits for them, and re-layouts  6.9 us

profile of v1, /device:TPU:2, one launch (start us, length us, event | category | flops | bytes accessed | tf_op | source)
XLA Modules:
  0.0 71.9 jit_solution(9285394486424150967)
XLA Ops:
  0.6 64.3 %shard_map.84 = (bf16[640,1024]{1,0:T(8,128)(2,1)}, f32[32,256]{1,0:T(8,128)}, bf16[2,1024,512]{2,1,0:T(8,128)(2,1)}, bf16[2,512,1024]{2,1,0:T(8,128)(2,1)}) custom-call(bf16[640,1024]{1,0:T(8,128)(2,1)} %bitcast.4, bf16[1024,256]{1,0:T(8,128)(2,1)} %keys_hbm.1, bf16[2,1024,512]{2,1,0:T(8,128)(2,1)} %wi_hbm.1, bf16[2,512,1024]{2,1,0:T(8,128)(2,1)} %wo_hbm.1, ...), custom_call_target="tpu_custom_call" | custom-call | flops 4000000000 | bytes 13000000 | tf_op jit(solution)/shard_map/pallas_call | solution.py:517
  64.9 0.0 copy-start.2
  64.9 0.0 copy-start.1
  65.0 2.6 %copy.13 = bf16[1,640,1024]{2,1,0:T(8,128)(2,1)} copy(bf16[1,640,1024]{2,1,0:T(8,128)(2,1)} %bitcast.3) | data formatting | bytes 2621440
  67.6 0.0 copy-done.2
  67.6 0.6 copy.14
  68.2 0.0 copy-done.1
  68.2 0.0 copy-start
  68.2 1.3 %copy.15 = bf16[2,1024,512]{2,1,0:T(8,128)(2,1)} copy(bf16[2,1024,512]{2,1,0:T(8,128)(2,1)S(1)} %copy-done.1) | data formatting | bytes 4194304
  69.5 1.0 %copy-done = bf16[2,512,1024]{2,1,0:T(8,128)(2,1)S(1)} copy-done((bf16[2,512,1024]{2,1,0:T(8,128)(2,1)S(1)}, bf16[2,512,1024]{2,1,0:T(8,128)(2,1)}, u32[]{:S(2)}) %copy-start) | copy-done | bytes 2097176
  70.5 1.3 %copy.16 = bf16[2,512,1024]{2,1,0:T(8,128)(2,1)} copy(bf16[2,512,1024]{2,1,0:T(8,128)(2,1)S(1)} %copy-done) | data formatting | bytes 4194304
Async XLA Ops:
  64.9 2.6 %copy-start.2 = (f32[32,256]{1,0:T(8,128)S(1)}, f32[32,256]{1,0:T(8,128)}, u32[]{:S(2)}) copy-start(f32[32,256]{1,0:T(8,128)} %get-tuple-element.17) | copy-start | bytes 98308
  64.9 3.2 %copy-start.1 = (bf16[2,1024,512]{2,1,0:T(8,128)(2,1)S(1)}, bf16[2,1024,512]{2,1,0:T(8,128)(2,1)}, u32[]{:S(2)}) copy-start(bf16[2,1024,512]{2,1,0:T(8,128)(2,1)} %get-tuple-element.18) | copy-start | bytes 6291460
  68.2 2.3 %copy-start = (bf16[2,512,1024]{2,1,0:T(8,128)(2,1)S(1)}, bf16[2,512,1024]{2,1,0:T(8,128)(2,1)}, u32[]{:S(2)}) copy-start(bf16[2,512,1024]{2,1,0:T(8,128)(2,1)} %get-tuple-element.19) | copy-start | bytes 6291460

commit v2 on v1

v2 whole, which is shorter than its diff:
```python
import jax
import jax.numpy as jnp
from jax import lax
from jax.experimental import pallas as pl
from jax.experimental.pallas import tpu as pltpu
from jax.sharding import PartitionSpec as P

MESH = pl.DeviceIdType.MESH
BF = jnp.bfloat16
F32 = jnp.float32

T = 640
D = 1024
S = 256
HL = 512
NZ = 8
SIDE = 4
NC = SIDE * SIDE

PLANE = sorted(range(1, NC), key=lambda d: -sum(min(i, SIDE - i) for i in divmod(d, SIDE)))
LINE = sorted(range(1, NZ), key=lambda e: -min(e, NZ - e))

GELU_A = 0.7978845608028654
GELU_B = 0.044715


def gelu_value(value):
    return 0.5 * value * (1.0 + jnp.tanh(GELU_A * (value + GELU_B * value * value * value)))


def gelu_slope(value):
    inner = jnp.tanh(GELU_A * (value + GELU_B * value * value * value))
    return 0.5 * (1.0 + inner) + 0.5 * value * (1.0 - inner * inner) * GELU_A * (
        1.0 + 3.0 * GELU_B * value * value
    )


def nn(a, b):
    return lax.dot_general(a, b, (((1,), (0,)), ((), ())), preferred_element_type=F32)


def nt(a, b):
    return lax.dot_general(a, b, (((1,), (1,)), ((), ())), preferred_element_type=F32)


def tn(a, b):
    return lax.dot_general(a, b, (((0,), (0,)), ((), ())), preferred_element_type=F32)


def fold(rows):
    return jnp.concatenate([rows[:, : D // 2], rows[:, D // 2 :]], axis=0)


def unfold(rows):
    return jnp.concatenate([rows[:8], rows[8:]], axis=1)


def add_all(acc, ref, n):
    for i in range(1, n):
        acc = acc + ref[i].astype(F32)
    return acc


def lanes(shape, columns):
    at = lax.broadcasted_iota(jnp.int32, shape, 1)
    tile = jnp.zeros(shape, F32)
    for i, column in enumerate(columns):
        tile = jnp.where(at == i, column, tile)
    return tile


def split2(value):
    high = value.astype(BF).astype(F32)
    return high, value - high


class Copies:
    def __init__(self, open_copies, make, low, high):
        self.make, self.low, self.high = make, low, high
        self.order = {NC: PLANE, NZ: LINE}.get(high, [0])
        self.sent = self.received = True
        open_copies.append(self)

    def start(self, d):
        self.sent = self.received = False
        self.make(d).start()

    def start_all(self):
        for d in self.order:
            self.start(d)

    def wait_recv(self, d):
        self.received = True
        self.make(d).wait_recv()

    def wait_recv_all(self):
        loop(self.low, self.high, self.wait_recv)

    def wait_send(self, d):
        self.make(d).wait_send()

    def drain(self):
        if not self.received:
            self.wait_recv_all()
        if not self.sent:
            loop(self.low, self.high, self.wait_send)


class Local:
    def __init__(self, open_copies, *copy):
        self.copy = pltpu.make_async_copy(*copy)
        self.waited = True
        open_copies.append(self)

    def start(self):
        self.waited = False
        self.copy.start()

    def wait(self):
        self.waited = True
        self.copy.wait()

    def drain(self):
        if not self.waited:
            self.wait()


def loop(low, high, body):
    def step(i, carry):
        body(i)
        return carry

    lax.fori_loop(low, high, step, 0)


def kernel(
    x_hbm, keys_hbm, wi_hbm, wo_hbm, g_hbm,
    tgs, kout, wigs, wogs,
    x, keys, wi, wo, g,
    keysT, LT, comb, combH, disp, xT,
    gs_send, gs_recv, gsum, gpk, garr,
    us_send, us_recv, usum, ustat, upk, uarr,
    rown, zg, zu, gall, rall, pre, act, pg, outp,
    cpk, crecv, bpk, brecv,
    so, si, sof, sif, cpart, lgH, lgN, dispH,
    ks_send, ks_recv, ksum, kpk, karr, kz, kzarr,
    ld, sib_s, sib_r,
    ag_s, ag_r, au_s, au_r,
    bg_s, bg_r, bu_s, bu_r,
    co_s, co_r, cb_s, cb_r,
    do_s, do_r, db_s, db_r, fo_s, fo_r, fb_s, fb_r,
    fk_s, fk_r, fz_s, fz_r,
):
    dp = lax.axis_index("dp")
    ctx = lax.axis_index("ctx")
    core = lax.rem(ctx, 2)
    chip = lax.div(ctx, 2)
    cy, cx = lax.div(chip, SIDE), lax.rem(chip, SIDE)
    other = 1 - core
    sib = {"ctx": chip * 2 + other}

    def ahead(d):
        return lax.rem(cy + d // SIDE, SIDE) * SIDE + lax.rem(cx + d % SIDE, SIDE)

    def behind(d):
        return (
            lax.rem(cy + SIDE - d // SIDE, SIDE) * SIDE
            + lax.rem(cx + SIDE - d % SIDE, SIDE)
        )

    def zahead(e):
        return lax.rem(dp + e, NZ)

    def zbehind(e):
        return lax.rem(dp + NZ - e, NZ)

    open_copies = []

    def remote(src, dst, send, recv, device):
        return pltpu.make_async_remote_copy(
            src_ref=src, dst_ref=dst, send_sem=send, recv_sem=recv,
            device_id=device, device_id_type=MESH,
        )

    load_keys = Local(open_copies, keys_hbm, keys, ld.at[0])
    parts = (slice(0, 256), slice(256, 512), slice(512, T))
    load_x = [Local(open_copies, x_hbm.at[at], x.at[at], ld.at[5 + i]) for i, at in enumerate(parts)]
    load_g = Local(open_copies, g_hbm, g, ld.at[2])
    load_wo = Local(open_copies, wo_hbm, wo, ld.at[3])
    load_wi = Local(open_copies, wi_hbm, wi, ld.at[4])
    for copy in (load_keys, *load_x, load_g):
        copy.start()

    barrier = pltpu.get_barrier_semaphore()
    pl.semaphore_signal(barrier, inc=1, device_id=sib, device_id_type=MESH)

    def greet_plane(d):
        pl.semaphore_signal(
            barrier, inc=1, device_id={"ctx": ahead(d) * 2 + core}, device_id_type=MESH
        )

    loop(1, NC, greet_plane)

    def greet_z(e):
        pl.semaphore_signal(barrier, inc=1, device_id={"dp": zahead(e)}, device_id_type=MESH)

    loop(1, NZ, greet_z)

    load_keys.wait()
    for b in range(D // 128):
        block = keys[b * 128 : (b + 1) * 128, :].astype(F32).T
        keysT[:, b * 128 : (b + 1) * 128] = jnp.concatenate(
            [block[(2 * j + k) * 8 : (2 * j + k) * 8 + 8] for k in range(2) for j in range(NC)], axis=0
        ).astype(BF)
    for copy, part in zip(load_x, parts):
        copy.wait()
        LT[:, part] = nt(keysT[...], x[part, :])
        for t in range(part.start // 128, part.stop // 128):
            at = slice(t * 128, (t + 1) * 128)
            logit = LT[:, at]
            e = jnp.exp(logit - jnp.max(logit, axis=0, keepdims=True))
            e = e / jnp.sum(e, axis=0, keepdims=True)
            comb[:, at] = e
            combH[:, at] = e.astype(BF)
    load_g.wait()
    mine = pl.ds(pl.multiple_of(core * 128, 128), 128)
    theirs = pl.ds(pl.multiple_of(other * 128, 128), 128)
    gs_send[...] = nn(combH[theirs, :], g[...]).astype(BF)
    pl.semaphore_wait(barrier, NC + NZ - 1)
    sib_g = Copies(open_copies, lambda d: remote(gs_send, gs_recv, sib_s.at[0], sib_r.at[0], sib), 0, 1)
    sib_g.start(0)
    load_wo.start()
    load_wi.start()

    logit = LT[...]
    top = jnp.max(logit, axis=1, keepdims=True).astype(BF).astype(F32)
    e = jnp.exp(logit - top)
    total = jnp.sum(e, axis=1, keepdims=True)
    disp[...] = e.astype(BF)
    high, low = split2(total)
    ustat[...] = lanes((S, 128), (top, high, low))
    us_send[:, :D] = nn(disp[theirs, :], x[...]).astype(BF)
    us_send[:, D:] = ustat[theirs, :].astype(BF)
    sib_u = Copies(open_copies, lambda d: remote(us_send, us_recv, sib_s.at[1], sib_r.at[1], sib), 0, 1)
    sib_u.start(0)
    gsum[...] = nn(combH[mine, :], g[...])
    usum[...] = nn(disp[mine, :], x[...])

    sib_g.wait_recv(0)
    gsum[...] += gs_recv[...].astype(F32)

    def ag_copy(d):
        j = ahead(d)
        return remote(gpk.at[j], garr.at[d], ag_s.at[d], ag_r.at[d], {"ctx": j * 2 + core})

    ag = Copies(open_copies, ag_copy, 1, NC)

    def send_g(d):
        j = ahead(d)
        gpk[j] = fold(gsum[pl.ds(pl.multiple_of(j * 8, 8), 8), :]).astype(BF)
        ag.start(d)

    for d in PLANE:
        send_g(d)

    own = ustat[mine, :]
    sib_u.wait_recv(0)
    got = us_recv[:, D:].astype(F32)
    top_a, top_b = own[:, 0:1], got[:, 0:1]
    top = jnp.maximum(top_a, top_b)
    wa, wb = jnp.exp(top_a - top), jnp.exp(top_b - top)
    total = (own[:, 1:2] + own[:, 2:3]) * wa + (got[:, 1:2] + got[:, 2:3]) * wb
    usum[...] = usum[...] * wa + us_recv[:, :D].astype(F32) * wb
    high, low = split2(total)
    ustat[0:128, :] = lanes((128, 128), (top, high, low))

    def pack_u(j):
        at = pl.ds(pl.multiple_of(j * 8, 8), 8)
        s = ustat[at, :]
        return jnp.concatenate([fold(usum[at, :]), jnp.concatenate([s, s], axis=0)], axis=1)

    def au_copy(d):
        j = ahead(d)
        return remote(upk.at[j], uarr.at[d], au_s.at[d], au_r.at[d], {"ctx": j * 2 + core})

    au = Copies(open_copies, au_copy, 1, NC)

    def send_u(d):
        j = ahead(d)
        upk[j] = pack_u(j).astype(BF)
        au.start(d)

    for d in PLANE:
        send_u(d)

    for b in range(D // 128):
        block = x[:, b * 128 : (b + 1) * 128].astype(F32).T.astype(BF)
        xT[0, b * 64 : (b + 1) * 64, :] = jnp.concatenate([block[0:32], block[64:96]], axis=0)
        xT[1, b * 64 : (b + 1) * 64, :] = jnp.concatenate([block[32:64], block[96:128]], axis=0)

    acc = fold(gsum[pl.ds(pl.multiple_of(chip * 8, 8), 8), :])
    ag.wait_recv_all()
    zg[dp] = add_all(acc, garr, NC).astype(BF)

    def bg_copy(e):
        return remote(zg.at[dp], zg.at[dp], bg_s.at[e], bg_r.at[e], {"dp": zahead(e)})

    bg = Copies(open_copies, bg_copy, 1, NZ)

    bg.start_all()

    uarr[0] = pack_u(chip).astype(BF)
    half = D // 2

    au.wait_recv_all()
    stats = uarr[:, :, half : half + 128].astype(F32)
    top = jnp.max(stats[:, :, 0:1], axis=0)
    w = jnp.exp(stats[:, :, 0:1] - top)
    total = jnp.sum(w * (stats[:, :, 1:2] + stats[:, :, 2:3]), axis=0)
    acc = jnp.zeros((16, half), F32)
    for d in range(NC):
        acc = acc + w[d] * uarr[d, :, :half].astype(F32)
    acc = acc / total
    rown[...] = acc
    zu[dp] = acc.astype(BF)

    def bu_copy(e):
        return remote(zu.at[dp], zu.at[dp], bu_s.at[e], bu_r.at[e], {"dp": zahead(e)})

    bu = Copies(open_copies, bu_copy, 1, NZ)

    bu.start_all()

    first = lax.rem(lax.broadcasted_iota(jnp.int32, (64, HL), 0), 8) < 4
    bg.wait_recv_all()
    gall[...] = jnp.concatenate([unfold(zg[c].astype(F32)) for c in range(NZ)], axis=0).astype(BF)
    load_wo.wait()
    act_grad = jnp.where(first, nt(gall[...], wo[0]), nt(gall[...], wo[1]))
    pre[...] = act_grad
    bu.wait_recv_all()
    rall[...] = jnp.concatenate([unfold(zu[c].astype(F32)) for c in range(NZ)], axis=0).astype(BF)
    load_wi.wait()
    pre_act = jnp.where(first, nn(rall[...], wi[0]), nn(rall[...], wi[1]))
    a = gelu_value(pre_act)
    act[0] = jnp.where(first, a, 0.0).astype(BF)
    act[1] = jnp.where(first, 0.0, a).astype(BF)
    p = pre[...] * gelu_slope(pre_act)
    pg[0] = jnp.where(first, p, 0.0).astype(BF)
    pg[1] = jnp.where(first, 0.0, p).astype(BF)

    def co_copy(e):
        j = zahead(e)
        return remote(cpk.at[j], crecv.at[e], co_s.at[e], co_r.at[e], {"dp": j})

    co = Copies(open_copies, co_copy, 1, NZ)

    def cb_copy(e):
        j = zahead(e)
        return remote(bpk.at[j], brecv.at[e], cb_s.at[e], cb_r.at[e], {"dp": j})

    cb = Copies(open_copies, cb_copy, 1, NZ)

    def clip_rows(j):
        return fold(outp[pl.ds(pl.multiple_of(j * 8, 8), 8), :])

    def send_o(e):
        j = zahead(e)
        cpk[j] = clip_rows(j).astype(BF)
        co.start(e)

    outp[...] = nn(act[0], wo[0]) + nn(act[1], wo[1])
    for d in LINE:
        send_o(d)
    o_own = clip_rows(dp)

    def send_b(e):
        j = zahead(e)
        bpk[j] = clip_rows(j).astype(BF)
        cb.start(e)

    outp[...] = nt(pg[0], wi[0]) + nt(pg[1], wi[1])
    for d in LINE:
        send_b(d)
    b_own = clip_rows(dp)

    for e in range(2):
        for c in range(HL // 128):
            at = slice(c * 128, (c + 1) * 128)
            wogs[e, at, :] = tn(act[e, :, at], gall[...]).astype(BF)

    co.wait_recv_all()
    so[core, chip] = add_all(o_own, crecv, NZ).astype(BF)

    def do_copy(d):
        return remote(
            so.at[core, chip], so.at[core, chip], do_s.at[d], do_r.at[d], {"ctx": ahead(d) * 2 + core}
        )

    do = Copies(open_copies, do_copy, 1, NC)

    def fo_copy(d):
        j = behind(d)
        return remote(so.at[core, j], so.at[core, j], fo_s.at[d], fo_r.at[d], sib)

    fo = Copies(open_copies, fo_copy, 0, NC)


    do.start_all()
    fo.start(0)

    cb.wait_recv_all()
    back = add_all(b_own, brecv, NZ).astype(BF)
    si[core, chip, :, :half] = back
    inner = jnp.sum(rown[...] * back.astype(F32), axis=1, keepdims=True)
    inner = inner[:8] + inner[8:]
    inner = jnp.concatenate([inner, inner], axis=0)
    z_high, z_low = split2(total)
    i_high, i_low = split2(inner)
    si[core, chip, :, half:] = lanes((16, 128), (top, z_high, z_low, i_high, i_low)).astype(BF)

    def db_copy(d):
        return remote(
            si.at[core, chip], si.at[core, chip], db_s.at[d], db_r.at[d], {"ctx": ahead(d) * 2 + core}
        )

    db = Copies(open_copies, db_copy, 1, NC)

    def fb_copy(d):
        j = behind(d)
        return remote(si.at[core, j], si.at[core, j], fb_s.at[d], fb_r.at[d], sib)

    fb = Copies(open_copies, fb_copy, 0, NC)


    db.start_all()
    fb.start(0)

    def pass_o(d):
        do.wait_recv(d)
        fo.start(d)

    loop(1, NC, pass_o)

    def pass_b(d):
        db.wait_recv(d)
        fb.start(d)

    for e in range(2):
        for c in range(D // 128):
            at = slice(c * 128, (c + 1) * 128)
            wigs[e, at, :] = tn(rall[:, at], pg[e]).astype(BF)

    loop(1, NC, pass_b)
    fo.wait_recv_all()

    def rows_of(ref, k, q):
        return jnp.concatenate(
            [unfold(ref[k, 2 * q, :, :half].astype(F32)), unfold(ref[k, 2 * q + 1, :, :half].astype(F32))],
            axis=0,
        ).astype(BF)

    for k in range(2):
        for q in range(NC // 2):
            at = k * 128 + q * 16
            sof[at : at + 16, :] = rows_of(so, k, q)
    cpart[...] = nt(sof[...], g[...])
    for t in range(T // 128):
        at = slice(t * 128, (t + 1) * 128)
        prob, back = comb[:, at], cpart[:, at]
        cpart[:, at] = prob * (back - jnp.sum(prob * back, axis=0, keepdims=True))

    fb.wait_recv_all()
    for k in range(2):
        for q in range(NC // 2):
            at = k * 128 + q * 16
            sif[at : at + 16, :] = rows_of(si, k, q)
    stat = jnp.concatenate(
        [si[k, j, 0:8, half : half + 128].astype(F32) for k in range(2) for j in range(NC)], axis=0
    )
    top = stat[:, 0:1]
    over = 1.0 / (stat[:, 1:2] + stat[:, 2:3])
    inner = stat[:, 3:4] + stat[:, 4:5]
    comb[...] = nt(sif[...], x[...])
    for t in range(T // 128):
        at = slice(t * 128, (t + 1) * 128)
        prob = jnp.exp(LT[:, at] - top) * over
        dispH[:, at] = prob.astype(BF)
        lg = prob * (comb[:, at] - inner) + cpart[:, at]
        lgH[:, at] = lg.astype(BF)
        lgN[:, at] = jnp.concatenate(
            [lg[k * 128 + j * 8 : k * 128 + j * 8 + 8] for j in range(NC) for k in range(2)], axis=0
        ).astype(BF)

    ks_send[...] = nt(xT[other], lgN[...]).astype(BF)
    sib_k = Copies(open_copies, lambda d: remote(ks_send, ks_recv, sib_s.at[2], sib_r.at[2], sib), 0, 1)
    sib_k.start(0)
    ksum[...] = nt(xT[core], lgN[...])
    sib_k.wait_recv(0)
    ksum[...] += ks_recv[...].astype(F32)

    def fk_copy(d):
        j = ahead(d)
        return remote(kpk.at[j], karr.at[d], fk_s.at[d], fk_r.at[d], {"ctx": j * 2 + core})

    fk = Copies(open_copies, fk_copy, 1, NC)

    def key_rows(j):
        return ksum[pl.ds(pl.multiple_of(j * 32, 32), 32), :]

    def send_k(d):
        j = ahead(d)
        kpk[j] = key_rows(j).astype(BF)
        fk.start(d)

    for d in PLANE:
        send_k(d)

    for t in range(T // 128):
        at = slice(t * 128, (t + 1) * 128)
        tgs[at, :] = (tn(lgH[:, at], keysT[...]) + tn(dispH[:, at], sif[...])).astype(BF)

    fk.wait_recv_all()
    acc = add_all(key_rows(chip), karr, NC)
    kz[...] = acc.astype(BF)

    def fz_copy(e):
        return remote(kz, kzarr.at[e], fz_s.at[e], fz_r.at[e], {"dp": zahead(e)})

    fz = Copies(open_copies, fz_copy, 1, NZ)


    fz.start_all()

    fz.wait_recv_all()
    kout[...] = add_all(acc, kzarr, NZ)

    for copies in open_copies:
        copies.drain()


def store_kernel(tgs, kout, wigs, wogs, tg_hbm, kg_hbm, wig_hbm, wog_hbm, st):
    pairs = ((wigs, wig_hbm), (wogs, wog_hbm), (tgs, tg_hbm), (kout, kg_hbm))
    copies = [pltpu.make_async_copy(src, dst, st.at[i]) for i, (src, dst) in enumerate(pairs)]
    for copy in copies:
        copy.start()
    for copy in copies:
        copy.wait()


def per_device(tokens, slot_keys, w_in, w_out, out_grad):
    hbm = pl.BlockSpec(memory_space=pltpu.HBM)
    vmem = pltpu.VMEM
    half = D // 2
    plane, line = pltpu.SemaphoreType.DMA((NC,)), pltpu.SemaphoreType.DMA((NZ,))
    held = pl.pallas_call(
        kernel,
        out_shape=(
            pltpu.VMEM((T, D), BF),
            pltpu.VMEM((32, S), F32),
            pltpu.VMEM((2, D, HL), BF),
            pltpu.VMEM((2, HL, D), BF),
        ),
        in_specs=[hbm] * 5,
        out_specs=(pl.BlockSpec(memory_space=vmem),) * 4,
        scratch_shapes=[
            vmem((T, D), BF), vmem((D, S), BF), vmem((2, D, HL), BF), vmem((2, HL, D), BF), vmem((T, D), BF),
            vmem((S, D), BF), vmem((S, T), F32), vmem((S, T), F32), vmem((S, T), BF), vmem((S, T), BF),
            vmem((2, D // 2, T), BF),
            vmem((128, D), BF), vmem((128, D), BF), vmem((128, D), F32),
            vmem((NC, 16, half), BF), vmem((NC, 16, half), BF),
            vmem((128, D + 128), BF), vmem((128, D + 128), BF), vmem((128, D), F32), vmem((S, 128), F32),
            vmem((NC, 16, half + 128), BF), vmem((NC, 16, half + 128), BF),
            vmem((16, half), F32), vmem((NZ, 16, half), BF), vmem((NZ, 16, half), BF),
            vmem((64, D), BF), vmem((64, D), BF), vmem((64, HL), F32),
            vmem((2, 64, HL), BF), vmem((2, 64, HL), BF), vmem((64, D), F32),
            vmem((NZ, 16, half), BF), vmem((NZ, 16, half), BF),
            vmem((NZ, 16, half), BF), vmem((NZ, 16, half), BF),
            vmem((2, NC, 16, half), BF), vmem((2, NC, 16, half + 128), BF), vmem((S, D), BF), vmem((S, D), BF),
            vmem((S, T), F32), vmem((S, T), BF), vmem((S, T), BF), vmem((S, T), BF),
            vmem((D // 2, S), BF), vmem((D // 2, S), BF), vmem((D // 2, S), F32),
            vmem((NC, 32, S), BF), vmem((NC, 32, S), BF), vmem((32, S), BF), vmem((NZ, 32, S), BF),
            pltpu.SemaphoreType.DMA((8,)),
            pltpu.SemaphoreType.DMA((3,)), pltpu.SemaphoreType.DMA((3,)),
            plane, plane, plane, plane,
            line, line, line, line,
            line, line, line, line,
            plane, plane, plane, plane, plane, plane, plane, plane,
            plane, plane, line, line,
        ],
        compiler_params=pltpu.CompilerParams(
            collective_id=0, has_side_effects=True, vmem_limit_bytes=36 * 2**20
        ),
        cost_estimate=pl.CostEstimate(flops=4 * 10**9, bytes_accessed=13 * 10**6, transcendentals=10**6),
    )(*(pltpu.with_memory_space_constraint(a, pltpu.HBM) for a in (tokens[0], slot_keys, w_in, w_out, out_grad[0])))
    tg, kg, wig, wog = pl.pallas_call(
        store_kernel,
        out_shape=(
            pltpu.HBM((T, D), BF),
            pltpu.HBM((32, S), F32),
            pltpu.HBM((2, D, HL), BF),
            pltpu.HBM((2, HL, D), BF),
        ),
        in_specs=[pl.BlockSpec(memory_space=vmem)] * 4,
        out_specs=(hbm,) * 4,
        scratch_shapes=[pltpu.SemaphoreType.DMA((4,))],
        compiler_params=pltpu.CompilerParams(vmem_limit_bytes=2**20),
    )(*held)
    return tg[None], kg, wig, wog


def solution(mesh):
    return jax.shard_map(
        per_device,
        mesh=mesh,
        in_specs=(
            P("dp", "ctx", None),
            P(),
            P("ctx", None, "dp"),
            P("ctx", "dp", None),
            P("dp", "ctx", None),
        ),
        out_specs=(
            P("dp", "ctx", None),
            P("ctx", None),
            P("ctx", None, "dp"),
            P("ctx", "dp", None),
        ),
        check_vma=False,
    )
```

time: 72.2 us -> 61.8 us (0.86)
  local copies, waits for them, and re-layouts: 6.9 us -> 0 us
  Pallas kernels: 64.3 us -> 61.1 us
    unnamed x10 -> x0, local copies, waits for them, and re-layouts: 6.9 us -> none
    pallas_call x1 -> x2, Pallas kernels: 64.3 us -> 61.1 us  [the longest x1 58.6 us: per_device(): pl.pallas_call(kernel, out_shape=(pltpu.VMEM((T, D), BF), pltpu.VMEM((32,...]
where the time goes in v2:
time: 61.8 us; the launch traced here: 61.7 us
  Pallas kernels  61.1 us (99%)
  between operations  0.64 us (1%)
    pallas_call x1, Pallas kernels, per_device(): pl.pallas_call(kernel, out_shape=(pltpu.VMEM((T, D), BF), pltpu.VMEM((32,...  58.6 us
    pallas_call x1, Pallas kernels, per_device(): pl.pallas_call(store_kernel, out_shape=(pltpu.HBM((T, D), BF), pltpu.HBM(...  2.48 us

profile of v2, /device:TPU:2, one launch (start us, length us, event | category | flops | bytes accessed | tf_op | source)
XLA Modules:
  0.0 61.7 jit_solution(11108823456577448215)
XLA Ops:
  0.6 58.6 %shard_map.84 = (bf16[640,1024]{1,0:T(8,128)(2,1)S(1)}, f32[32,256]{1,0:T(8,128)S(1)}, bf16[2,1024,512]{2,1,0:T(8,128)(2,1)S(1)}, bf16[2,512,1024]{2,1,0:T(8,128)(2,1)S(1)}) custom-call(bf16[640,1024]{1,0:T(8,128)(2,1)} %bitcast.3, bf16[1024,256]{1,0:T(8,128)(2,1)} %keys_hbm.1, bf16[2,1024,512]{2,1,0:T(8,128)(2,1)} %wi_hbm.1, bf16[2,512,1024]{2,1,0:T(8,128)(2,1)} %wo_hbm.1, ...), custom_call_target="tpu_custom_call" | custom-call | flops 4000000000 | bytes 13000000 | tf_op jit(solution)/shard_map/pallas_call | solution.py:555
  59.2 2.5 %shard_map.85 = (bf16[640,1024]{1,0:T(8,128)(2,1)}, f32[32,256]{1,0:T(8,128)}, bf16[2,1024,512]{2,1,0:T(8,128)(2,1)}, bf16[2,512,1024]{2,1,0:T(8,128)(2,1)}) custom-call(bf16[640,1024]{1,0:T(8,128)(2,1)S(1)} %get-tuple-element.12.tgs, f32[32,256]{1,0:T(8,128)S(1)} %get-tuple-element.13.kout, bf16[2,1024,512]{2,1,0:T(8,128)(2,1)S(1)} %get-tuple-element.14.wigs, ...), custom_call_target="tpu_custom_call" | custom-call | tf_op jit(solution)/shard_map/pallas_call | solution.py:595

commit v3 on v2

v3 whole, which is shorter than its diff:
```python
import jax
import jax.numpy as jnp
from jax import lax
from jax.experimental import pallas as pl
from jax.experimental.pallas import tpu as pltpu
from jax.sharding import PartitionSpec as P

MESH = pl.DeviceIdType.MESH
BF = jnp.bfloat16
F32 = jnp.float32

T = 640
D = 1024
S = 256
HL = 512
NZ = 8
SIDE = 4
NC = SIDE * SIDE

PLANE = sorted(range(1, NC), key=lambda d: -sum(min(i, SIDE - i) for i in divmod(d, SIDE)))
LINE = sorted(range(1, NZ), key=lambda e: -min(e, NZ - e))

GELU_A = 0.7978845608028654
GELU_B = 0.044715


def gelu_value(value):
    return 0.5 * value * (1.0 + jnp.tanh(GELU_A * (value + GELU_B * value * value * value)))


def gelu_slope(value):
    inner = jnp.tanh(GELU_A * (value + GELU_B * value * value * value))
    return 0.5 * (1.0 + inner) + 0.5 * value * (1.0 - inner * inner) * GELU_A * (
        1.0 + 3.0 * GELU_B * value * value
    )


def nn(a, b):
    return lax.dot_general(a, b, (((1,), (0,)), ((), ())), preferred_element_type=F32)


def nt(a, b):
    return lax.dot_general(a, b, (((1,), (1,)), ((), ())), preferred_element_type=F32)


def tn(a, b):
    return lax.dot_general(a, b, (((0,), (0,)), ((), ())), preferred_element_type=F32)


def fold(rows):
    return jnp.concatenate([rows[:, : D // 2], rows[:, D // 2 :]], axis=0)


def unfold(rows):
    return jnp.concatenate([rows[:8], rows[8:]], axis=1)


def add_all(acc, ref, n):
    for i in range(1, n):
        acc = acc + ref[i].astype(F32)
    return acc


def lanes(shape, columns):
    at = lax.broadcasted_iota(jnp.int32, shape, 1)
    tile = jnp.zeros(shape, F32)
    for i, column in enumerate(columns):
        tile = jnp.where(at == i, column, tile)
    return tile


def split2(value):
    high = value.astype(BF).astype(F32)
    return high, value - high


class Copies:
    def __init__(self, open_copies, make, order, sent, received=None):
        self.make, self.order, self.sent, self.received = make, order, sent, received
        self.to_send = self.to_receive = False
        open_copies.append(self)

    def start(self, d):
        self.to_send = self.to_receive = True
        self.make(d).start()

    def start_all(self):
        for d in self.order:
            self.start(d)

    def wait_recv(self):
        self.to_receive = False
        ref, sem = self.received
        pltpu.make_async_copy(ref, ref, sem).wait()

    def wait_one(self, d):
        self.to_receive = False
        self.make(d).wait_recv()

    def drain(self):
        if self.to_receive:
            if self.received is None:
                for d in self.order:
                    self.wait_one(d)
            else:
                self.wait_recv()
        if self.to_send:
            ref, sem = self.sent
            pltpu.make_async_copy(ref, ref, sem).wait()


class Local:
    def __init__(self, open_copies, *copy):
        self.copy = pltpu.make_async_copy(*copy)
        self.waited = True
        open_copies.append(self)

    def start(self):
        self.waited = False
        self.copy.start()

    def wait(self):
        self.waited = True
        self.copy.wait()

    def drain(self):
        if not self.waited:
            self.wait()


def kernel(
    x_hbm, keys_hbm, wi_hbm, wo_hbm, g_hbm,
    tgs, kout, wigs, wogs,
    x, keys, wi, wo, g,
    keysT, LT, comb, combH, disp, xT,
    gs_send, gs_recv, gsum, gpk, garr,
    us_send, us_recv, usum, ustat, upk, uarr,
    wiT, woT, rown, zg, zu, gall, rall, pre, act, pg, outp,
    cpk, crecv, bpk, brecv,
    so, si, sof, sif, cpart, lgH, lgN, dispH,
    ks_send, ks_recv, ksum, kpk, karr, kz, kzarr,
    ld, send, recv, do_r, db_r,
):
    dp = lax.axis_index("dp")
    ctx = lax.axis_index("ctx")
    core = lax.rem(ctx, 2)
    chip = lax.div(ctx, 2)
    cy, cx = lax.div(chip, SIDE), lax.rem(chip, SIDE)
    other = 1 - core
    sib = {"ctx": chip * 2 + other}

    def ahead(d):
        return lax.rem(cy + d // SIDE, SIDE) * SIDE + lax.rem(cx + d % SIDE, SIDE)

    def behind(d):
        return (
            lax.rem(cy + SIDE - d // SIDE, SIDE) * SIDE
            + lax.rem(cx + SIDE - d % SIDE, SIDE)
        )

    def zahead(e):
        return lax.rem(dp + e, NZ)

    def zbehind(e):
        return lax.rem(dp + NZ - e, NZ)

    open_copies = []

    def remote(src, dst, send, recv, device):
        return pltpu.make_async_remote_copy(
            src_ref=src, dst_ref=dst, send_sem=send, recv_sem=recv,
            device_id=device, device_id_type=MESH,
        )

    load_keys = Local(open_copies, keys_hbm, keys, ld.at[0])
    parts = (slice(0, 256), slice(256, 512), slice(512, T))
    load_x = [Local(open_copies, x_hbm.at[at], x.at[at], ld.at[5 + i]) for i, at in enumerate(parts)]
    load_g = Local(open_copies, g_hbm, g, ld.at[2])
    load_wo = Local(open_copies, wo_hbm, wo, ld.at[3])
    load_wi = Local(open_copies, wi_hbm, wi, ld.at[4])
    for copy in (load_keys, *load_x):
        copy.start()

    barrier = pltpu.get_barrier_semaphore()
    pl.semaphore_signal(barrier, inc=1, device_id=sib, device_id_type=MESH)

    for d in PLANE:
        pl.semaphore_signal(
            barrier, inc=1, device_id={"ctx": ahead(d) * 2 + core}, device_id_type=MESH
        )
    for e in LINE:
        pl.semaphore_signal(barrier, inc=1, device_id={"dp": zahead(e)}, device_id_type=MESH)

    load_keys.wait()
    load_g.start()
    for b in range(D // 128):
        block = keys[b * 128 : (b + 1) * 128, :].astype(F32).T
        keysT[:, b * 128 : (b + 1) * 128] = jnp.concatenate(
            [block[(2 * j + k) * 8 : (2 * j + k) * 8 + 8] for k in range(2) for j in range(NC)], axis=0
        ).astype(BF)
    for copy, part in zip(load_x, parts):
        copy.wait()
        LT[:, part] = nt(keysT[...], x[part, :])
    mine = pl.ds(pl.multiple_of(core * 128, 128), 128)
    theirs = pl.ds(pl.multiple_of(other * 128, 128), 128)
    half = D // 2

    logit = LT[...]
    top = jnp.max(logit, axis=1, keepdims=True).astype(BF).astype(F32)
    e = jnp.exp(logit - top)
    total = jnp.sum(e, axis=1, keepdims=True)
    disp[...] = e.astype(BF)
    high, low = split2(total)
    ustat[...] = lanes((S, 128), (top, high, low))
    us_send[:, :D] = nn(disp[theirs, :], x[...]).astype(BF)
    us_send[:, D:] = ustat[theirs, :].astype(BF)
    pl.semaphore_wait(barrier, NC + NZ - 1)
    sib_u = Copies(
        open_copies, lambda d: remote(us_send, us_recv, send.at[1], recv.at[1], sib), [0],
        (us_send, send.at[1]), (us_recv, recv.at[1]),
    )
    sib_u.start_all()

    for t in range(T // 128):
        at = slice(t * 128, (t + 1) * 128)
        logit = LT[:, at]
        e = jnp.exp(logit - jnp.max(logit, axis=0, keepdims=True))
        e = e / jnp.sum(e, axis=0, keepdims=True)
        comb[:, at] = e
        combH[:, at] = e.astype(BF)
    load_g.wait()
    gs_send[...] = nn(combH[theirs, :], g[...]).astype(BF)
    sib_g = Copies(
        open_copies, lambda d: remote(gs_send, gs_recv, send.at[0], recv.at[0], sib), [0],
        (gs_send, send.at[0]), (gs_recv, recv.at[0]),
    )
    sib_g.start_all()
    usum[...] = nn(disp[mine, :], x[...])

    own = ustat[mine, :]
    sib_u.wait_recv()
    got = us_recv[:, D:].astype(F32)
    top_a, top_b = own[:, 0:1], got[:, 0:1]
    top = jnp.maximum(top_a, top_b)
    wa, wb = jnp.exp(top_a - top), jnp.exp(top_b - top)
    total = (own[:, 1:2] + own[:, 2:3]) * wa + (got[:, 1:2] + got[:, 2:3]) * wb
    usum[...] = usum[...] * wa + us_recv[:, :D].astype(F32) * wb
    high, low = split2(total)
    ustat[0:128, :] = lanes((128, 128), (top, high, low))
    for j in range(NC):
        tile = ustat[j * 8 : j * 8 + 8, :]
        upk[j] = jnp.concatenate(
            [fold(usum[j * 8 : j * 8 + 8, :]), jnp.concatenate([tile, tile], axis=0)], axis=1
        ).astype(BF)

    def au_copy(d):
        j = ahead(d)
        return remote(upk.at[j], uarr.at[d], send.at[4], recv.at[4], {"ctx": j * 2 + core})

    au = Copies(open_copies, au_copy, PLANE, (upk.at[0 : NC - 1], send.at[4]), (uarr.at[1:NC], recv.at[4]))
    au.start_all()
    uarr[0] = upk[chip]

    gsum[...] = nn(combH[mine, :], g[...])
    sib_g.wait_recv()
    gsum[...] += gs_recv[...].astype(F32)

    def ag_copy(d):
        j = ahead(d)
        return remote(gpk.at[j], garr.at[d], send.at[3], recv.at[3], {"ctx": j * 2 + core})

    ag = Copies(open_copies, ag_copy, PLANE, (gpk.at[0 : NC - 1], send.at[3]), (garr.at[1:NC], recv.at[3]))
    for j in range(NC):
        gpk[j] = fold(gsum[j * 8 : j * 8 + 8, :]).astype(BF)
    ag.start_all()
    load_wi.start()
    load_wo.start()

    for b in range(D // 128):
        block = x[:, b * 128 : (b + 1) * 128].T
        xT[0, b * 64 : (b + 1) * 64, :] = jnp.concatenate([block[0:32], block[64:96]], axis=0)
        xT[1, b * 64 : (b + 1) * 64, :] = jnp.concatenate([block[32:64], block[96:128]], axis=0)

    load_wi.wait()
    load_wo.wait()
    for e in range(2):
        for b in range(D // 128):
            at = slice(b * 128, (b + 1) * 128)
            wiT[e, :, at] = wi[e, at, :].T
        for b in range(HL // 128):
            at = slice(b * 128, (b + 1) * 128)
            woT[e, :, at] = wo[e, at, :].T

    au.wait_recv()
    stats = uarr[:, :, half : half + 128].astype(F32)
    top = jnp.max(stats[:, :, 0:1], axis=0)
    w = jnp.exp(stats[:, :, 0:1] - top)
    total = jnp.sum(w * (stats[:, :, 1:2] + stats[:, :, 2:3]), axis=0)
    acc = jnp.zeros((16, half), F32)
    for d in range(NC):
        acc = acc + w[d] * uarr[d, :, :half].astype(F32)
    acc = acc / total
    rown[...] = acc
    zu[dp] = acc.astype(BF)

    def bu_copy(e):
        return remote(zu.at[dp], zu.at[dp], send.at[6], recv.at[6], {"dp": zahead(e)})

    bu = Copies(open_copies, bu_copy, LINE, (zu.at[0 : NZ - 1], send.at[6]), (zu.at[0 : NZ - 1], recv.at[6]))
    bu.start_all()
    z_high, z_low = split2(total)
    so[core, chip, :, half:] = lanes((16, 128), (top, z_high, z_low)).astype(BF)

    acc = fold(gsum[pl.ds(pl.multiple_of(chip * 8, 8), 8), :])
    ag.wait_recv()
    zg[dp] = add_all(acc, garr, NC).astype(BF)

    def bg_copy(e):
        return remote(zg.at[dp], zg.at[dp], send.at[5], recv.at[5], {"dp": zahead(e)})

    bg = Copies(open_copies, bg_copy, LINE, (zg.at[0 : NZ - 1], send.at[5]), (zg.at[0 : NZ - 1], recv.at[5]))
    bg.start_all()

    first = lax.rem(lax.broadcasted_iota(jnp.int32, (64, HL), 0), 8) < 4
    bu.wait_recv()
    rall[...] = jnp.concatenate([unfold(zu[c].astype(F32)) for c in range(NZ)], axis=0).astype(BF)
    pre_act = jnp.where(first, nn(rall[...], wi[0]), nn(rall[...], wi[1]))
    a = gelu_value(pre_act)
    act[0] = jnp.where(first, a, 0.0).astype(BF)
    act[1] = jnp.where(first, 0.0, a).astype(BF)
    pre[...] = gelu_slope(pre_act)
    outp[...] = nn(act[0], wo[0]) + nn(act[1], wo[1])

    def co_copy(e):
        j = zahead(e)
        return remote(cpk.at[j], crecv.at[e], send.at[7], recv.at[7], {"dp": j})

    co = Copies(open_copies, co_copy, LINE, (cpk.at[0 : NZ - 1], send.at[7]), (crecv.at[1:NZ], recv.at[7]))
    for j in range(NZ):
        cpk[j] = fold(outp[j * 8 : j * 8 + 8, :]).astype(BF)
    co.start_all()
    o_own = fold(outp[pl.ds(pl.multiple_of(dp * 8, 8), 8), :])

    bg.wait_recv()
    gall[...] = jnp.concatenate([unfold(zg[c].astype(F32)) for c in range(NZ)], axis=0).astype(BF)
    p = jnp.where(first, nn(gall[...], woT[0]), nn(gall[...], woT[1])) * pre[...]
    pg[0] = jnp.where(first, p, 0.0).astype(BF)
    pg[1] = jnp.where(first, 0.0, p).astype(BF)
    outp[...] = nn(pg[0], wiT[0]) + nn(pg[1], wiT[1])

    def cb_copy(e):
        j = zahead(e)
        return remote(bpk.at[j], brecv.at[e], send.at[8], recv.at[8], {"dp": j})

    cb = Copies(open_copies, cb_copy, LINE, (bpk.at[0 : NZ - 1], send.at[8]), (brecv.at[1:NZ], recv.at[8]))
    for j in range(NZ):
        bpk[j] = fold(outp[j * 8 : j * 8 + 8, :]).astype(BF)
    cb.start_all()
    b_own = fold(outp[pl.ds(pl.multiple_of(dp * 8, 8), 8), :])

    co.wait_recv()
    so[core, chip, :, :half] = add_all(o_own, crecv, NZ).astype(BF)

    def do_copy(d):
        return remote(
            so.at[core, chip], so.at[core, chip], send.at[9], do_r.at[d], {"ctx": ahead(d) * 2 + core}
        )

    def fo_copy(d):
        j = behind(d)
        return remote(so.at[core, j], so.at[core, j], send.at[11], recv.at[11], sib)

    do = Copies(open_copies, do_copy, PLANE, (so.at[0, 0 : NC - 1], send.at[9]))
    fo = Copies(open_copies, fo_copy, [], (so.at[0], send.at[11]), (so.at[0], recv.at[11]))
    do.start_all()
    fo.start(0)

    for e in range(2):
        for c in range(HL // 128):
            at = slice(c * 128, (c + 1) * 128)
            wogs[e, at, :] = tn(act[e, :, at], gall[...]).astype(BF)
        for c in range(D // 128):
            at = slice(c * 128, (c + 1) * 128)
            wigs[e, at, :] = tn(rall[:, at], pg[e]).astype(BF)

    cb.wait_recv()
    back = add_all(b_own, brecv, NZ).astype(BF)
    si[core, chip, :, :half] = back
    inner = jnp.sum(rown[...] * back.astype(F32), axis=1, keepdims=True)
    inner = inner[:8] + inner[8:]
    inner = jnp.concatenate([inner, inner], axis=0)
    i_high, i_low = split2(inner)
    si[core, chip, :, half:] = lanes((16, 128), (i_high, i_low)).astype(BF)

    def db_copy(d):
        return remote(
            si.at[core, chip], si.at[core, chip], send.at[10], db_r.at[d], {"ctx": ahead(d) * 2 + core}
        )

    def fb_copy(d):
        j = behind(d)
        return remote(si.at[core, j], si.at[core, j], send.at[12], recv.at[12], sib)

    db = Copies(open_copies, db_copy, PLANE, (si.at[0, 0 : NC - 1], send.at[10]))
    fb = Copies(open_copies, fb_copy, [], (si.at[0], send.at[12]), (si.at[0], recv.at[12]))
    db.start_all()
    fb.start(0)

    for d in reversed(PLANE):
        do.wait_one(d)
        fo.start(d)

    def gather(ref, rows, k):
        for q in range(NC // 2):
            rows[pl.ds(pl.multiple_of(k * 128 + q * 16, 16), 16), :] = jnp.concatenate(
                [unfold(ref[k, 2 * q + i, :, :half].astype(F32)) for i in range(2)], axis=0
            ).astype(BF)

    def stat_of(ref):
        return jnp.concatenate(
            [ref[k, j, 0:8, half : half + 128].astype(F32) for k in range(2) for j in range(NC)], axis=0
        )

    gather(so, sof, core)
    cpart[mine, :] = nt(sof[mine, :], g[...])
    fo.wait_recv()
    gather(so, sof, other)
    cpart[theirs, :] = nt(sof[theirs, :], g[...])
    stat = stat_of(so)
    top = stat[:, 0:1]
    over = 1.0 / (stat[:, 1:2] + stat[:, 2:3])
    for t in range(T // 128):
        at = slice(t * 128, (t + 1) * 128)
        prob, back = comb[:, at], cpart[:, at]
        cpart[:, at] = prob * (back - jnp.sum(prob * back, axis=0, keepdims=True))
        prob = jnp.exp(LT[:, at] - top) * over
        LT[:, at] = prob
        dispH[:, at] = prob.astype(BF)

    for d in reversed(PLANE):
        db.wait_one(d)
        fb.start(d)
    gather(si, sif, core)
    comb[mine, :] = nt(sif[mine, :], x[...])
    fb.wait_recv()
    gather(si, sif, other)
    comb[theirs, :] = nt(sif[theirs, :], x[...])
    stat = stat_of(si)
    inner = stat[:, 0:1] + stat[:, 1:2]
    for t in range(T // 128):
        at = slice(t * 128, (t + 1) * 128)
        lg = LT[:, at] * (comb[:, at] - inner) + cpart[:, at]
        lgH[:, at] = lg.astype(BF)
        lgN[:, at] = jnp.concatenate(
            [lg[k * 128 + j * 8 : k * 128 + j * 8 + 8] for j in range(NC) for k in range(2)], axis=0
        ).astype(BF)

    ks_send[...] = nt(xT[other], lgN[...]).astype(BF)
    sib_k = Copies(
        open_copies, lambda d: remote(ks_send, ks_recv, send.at[2], recv.at[2], sib), [0],
        (ks_send, send.at[2]), (ks_recv, recv.at[2]),
    )
    sib_k.start_all()
    ksum[...] = nt(xT[core], lgN[...])
    sib_k.wait_recv()
    ksum[...] += ks_recv[...].astype(F32)

    def fk_copy(d):
        j = ahead(d)
        return remote(kpk.at[j], karr.at[d], send.at[13], recv.at[13], {"ctx": j * 2 + core})

    fk = Copies(open_copies, fk_copy, PLANE, (kpk.at[0 : NC - 1], send.at[13]), (karr.at[1:NC], recv.at[13]))

    for j in range(NC):
        kpk[j] = ksum[j * 32 : j * 32 + 32, :].astype(BF)
    fk.start_all()

    for t in range(T // 128):
        at = slice(t * 128, (t + 1) * 128)
        tgs[at, :] = (tn(lgH[:, at], keysT[...]) + tn(dispH[:, at], sif[...])).astype(BF)

    fk.wait_recv()
    acc = add_all(ksum[pl.ds(pl.multiple_of(chip * 32, 32), 32), :], karr, NC)
    kz[...] = acc.astype(BF)

    def fz_copy(e):
        return remote(kz, kzarr.at[e], send.at[14], recv.at[14], {"dp": zahead(e)})

    fz = Copies(open_copies, fz_copy, LINE, (kzarr.at[0 : NZ - 1], send.at[14]), (kzarr.at[1:NZ], recv.at[14]))


    fz.start_all()

    fz.wait_recv()
    kout[...] = add_all(acc, kzarr, NZ)

    for copies in open_copies:
        copies.drain()


def store_kernel(tgs, kout, wigs, wogs, tg_hbm, kg_hbm, wig_hbm, wog_hbm, st):
    pairs = ((wigs, wig_hbm), (wogs, wog_hbm), (tgs, tg_hbm), (kout, kg_hbm))
    copies = [pltpu.make_async_copy(src, dst, st.at[i]) for i, (src, dst) in enumerate(pairs)]
    for copy in copies:
        copy.start()
    for copy in copies:
        copy.wait()


def per_device(tokens, slot_keys, w_in, w_out, out_grad):
    hbm = pl.BlockSpec(memory_space=pltpu.HBM)
    vmem = pltpu.VMEM
    half = D // 2
    held = pl.pallas_call(
        kernel,
        out_shape=(
            pltpu.VMEM((T, D), BF),
            pltpu.VMEM((32, S), F32),
            pltpu.VMEM((2, D, HL), BF),
            pltpu.VMEM((2, HL, D), BF),
        ),
        in_specs=[hbm] * 5,
        out_specs=(pl.BlockSpec(memory_space=vmem),) * 4,
        scratch_shapes=[
            vmem((T, D), BF), vmem((D, S), BF), vmem((2, D, HL), BF), vmem((2, HL, D), BF), vmem((T, D), BF),
            vmem((S, D), BF), vmem((S, T), F32), vmem((S, T), F32), vmem((S, T), BF), vmem((S, T), BF),
            vmem((2, D // 2, T), BF),
            vmem((128, D), BF), vmem((128, D), BF), vmem((128, D), F32),
            vmem((NC, 16, half), BF), vmem((NC, 16, half), BF),
            vmem((128, D + 128), BF), vmem((128, D + 128), BF), vmem((128, D), F32), vmem((S, 128), F32),
            vmem((NC, 16, half + 128), BF), vmem((NC, 16, half + 128), BF),
            vmem((2, HL, D), BF), vmem((2, D, HL), BF),
            vmem((16, half), F32), vmem((NZ, 16, half), BF), vmem((NZ, 16, half), BF),
            vmem((64, D), BF), vmem((64, D), BF), vmem((64, HL), F32),
            vmem((2, 64, HL), BF), vmem((2, 64, HL), BF), vmem((64, D), F32),
            vmem((NZ, 16, half), BF), vmem((NZ, 16, half), BF),
            vmem((NZ, 16, half), BF), vmem((NZ, 16, half), BF),
            vmem((2, NC, 16, half + 128), BF), vmem((2, NC, 16, half + 128), BF), vmem((S, D), BF), vmem((S, D), BF),
            vmem((S, T), F32), vmem((S, T), BF), vmem((S, T), BF), vmem((S, T), BF),
            vmem((D // 2, S), BF), vmem((D // 2, S), BF), vmem((D // 2, S), F32),
            vmem((NC, 32, S), BF), vmem((NC, 32, S), BF), vmem((32, S), BF), vmem((NZ, 32, S), BF),
            pltpu.SemaphoreType.DMA((8,)), pltpu.SemaphoreType.DMA((15,)), pltpu.SemaphoreType.DMA((15,)),
            pltpu.SemaphoreType.DMA((NC,)), pltpu.SemaphoreType.DMA((NC,)),
        ],
        compiler_params=pltpu.CompilerParams(
            collective_id=0, has_side_effects=True, vmem_limit_bytes=36 * 2**20
        ),
        cost_estimate=pl.CostEstimate(flops=4 * 10**9, bytes_accessed=13 * 10**6, transcendentals=10**6),
    )(*(pltpu.with_memory_space_constraint(a, pltpu.HBM) for a in (tokens[0], slot_keys, w_in, w_out, out_grad[0])))
    tg, kg, wig, wog = pl.pallas_call(
        store_kernel,
        out_shape=(
            pltpu.HBM((T, D), BF),
            pltpu.HBM((32, S), F32),
            pltpu.HBM((2, D, HL), BF),
            pltpu.HBM((2, HL, D), BF),
        ),
        in_specs=[pl.BlockSpec(memory_space=vmem)] * 4,
        out_specs=(hbm,) * 4,
        scratch_shapes=[pltpu.SemaphoreType.DMA((4,))],
        compiler_params=pltpu.CompilerParams(vmem_limit_bytes=2**20),
    )(*held)
    return tg[None], kg, wig, wog


def solution(mesh):
    return jax.shard_map(
        per_device,
        mesh=mesh,
        in_specs=(
            P("dp", "ctx", None),
            P(),
            P("ctx", None, "dp"),
            P("ctx", "dp", None),
            P("dp", "ctx", None),
        ),
        out_specs=(
            P("dp", "ctx", None),
            P("ctx", None),
            P("ctx", None, "dp"),
            P("ctx", "dp", None),
        ),
        check_vma=False,
    )
```

time: 61.8 us -> 58.7 us (0.950)
  Pallas kernels: 61.1 us -> 57.4 us
    pallas_call x1, Pallas kernels: 58.6 us -> 54.9 us  [per_device(): pl.pallas_call(kernel, out_shape=(pltpu.VMEM((T, D), BF), pltpu.VMEM((32,...]
where the time goes in v3:
time: 58.7 us; the launch traced here: 58 us
  Pallas kernels  57.4 us (98%)
  between operations  0.64 us (1%)
    pallas_call x1, Pallas kernels, per_device(): pl.pallas_call(kernel, out_shape=(pltpu.VMEM((T, D), BF), pltpu.VMEM((32,...  54.9 us
    pallas_call x1, Pallas kernels, per_device(): pl.pallas_call(store_kernel, out_shape=(pltpu.HBM((T, D), BF), pltpu.HBM(...  2.48 us

profile of v3, /device:TPU:2, one launch (start us, length us, event | category | flops | bytes accessed | tf_op | source)
XLA Modules:
  0.0 58.0 jit_solution(8509818026731664482)
XLA Ops:
  0.6 54.9 %shard_map.84 = (bf16[640,1024]{1,0:T(8,128)(2,1)S(1)}, f32[32,256]{1,0:T(8,128)S(1)}, bf16[2,1024,512]{2,1,0:T(8,128)(2,1)S(1)}, bf16[2,512,1024]{2,1,0:T(8,128)(2,1)S(1)}) custom-call(bf16[640,1024]{1,0:T(8,128)(2,1)} %bitcast.3, bf16[1024,256]{1,0:T(8,128)(2,1)} %keys_hbm.1, bf16[2,1024,512]{2,1,0:T(8,128)(2,1)} %wi_hbm.1, bf16[2,512,1024]{2,1,0:T(8,128)(2,1)} %wo_hbm.1, ...), custom_call_target="tpu_custom_call" | custom-call | flops 4000000000 | bytes 13000000 | tf_op jit(solution)/shard_map/pallas_call | solution.py:514
  55.6 2.5 %shard_map.85 = (bf16[640,1024]{1,0:T(8,128)(2,1)}, f32[32,256]{1,0:T(8,128)}, bf16[2,1024,512]{2,1,0:T(8,128)(2,1)}, bf16[2,512,1024]{2,1,0:T(8,128)(2,1)}) custom-call(bf16[640,1024]{1,0:T(8,128)(2,1)S(1)} %get-tuple-element.12.tgs, f32[32,256]{1,0:T(8,128)S(1)} %get-tuple-element.13.kout, bf16[2,1024,512]{2,1,0:T(8,128)(2,1)S(1)} %get-tuple-element.14.wigs, ...), custom_call_target="tpu_custom_call" | custom-call | tf_op jit(solution)/shard_map/pallas_call | solution.py:550

commit v4 on v3

--- a/solution.py
+++ b/solution.py
@@ -134,12 +134,12 @@
     x, keys, wi, wo, g,
     keysT, LT, comb, combH, disp, xT,
     gs_send, gs_recv, gsum, gpk, garr,
-    us_send, us_recv, usum, ustat, upk, uarr,
+    us_send, us_recv, usum, ustat, upk, uarr, ust, ustr, utt,
     wiT, woT, rown, zg, zu, gall, rall, pre, act, pg, outp,
     cpk, crecv, bpk, brecv,
-    so, si, sof, sif, cpart, lgH, lgN, dispH,
+    so, si, sm, sof, sif, cpart, lgH, lgN, dispH,
     ks_send, ks_recv, ksum, kpk, karr, kz, kzarr,
-    ld, send, recv, do_r, db_r,
+    ld, send, recv, do_r, db_r, dm_r,
 ):
     dp = lax.axis_index("dp")
     ctx = lax.axis_index("ctx")
@@ -173,13 +173,12 @@
         )
 
     load_keys = Local(open_copies, keys_hbm, keys, ld.at[0])
-    parts = (slice(0, 256), slice(256, 512), slice(512, T))
-    load_x = [Local(open_copies, x_hbm.at[at], x.at[at], ld.at[5 + i]) for i, at in enumerate(parts)]
+    load_x = Local(open_copies, x_hbm, x, ld.at[1])
     load_g = Local(open_copies, g_hbm, g, ld.at[2])
     load_wo = Local(open_copies, wo_hbm, wo, ld.at[3])
     load_wi = Local(open_copies, wi_hbm, wi, ld.at[4])
-    for copy in (load_keys, *load_x):
-        copy.start()
+    load_keys.start()
+    load_x.start()
 
     barrier = pltpu.get_barrier_semaphore()
     pl.semaphore_signal(barrier, inc=1, device_id=sib, device_id_type=MESH)
@@ -198,9 +197,8 @@
         keysT[:, b * 128 : (b + 1) * 128] = jnp.concatenate(
             [block[(2 * j + k) * 8 : (2 * j + k) * 8 + 8] for k in range(2) for j in range(NC)], axis=0
         ).astype(BF)
-    for copy, part in zip(load_x, parts):
-        copy.wait()
-        LT[:, part] = nt(keysT[...], x[part, :])
+    load_x.wait()
+    LT[...] = nt(keysT[...], x[...])
     mine = pl.ds(pl.multiple_of(core * 128, 128), 128)
     theirs = pl.ds(pl.multiple_of(other * 128, 128), 128)
     half = D // 2
@@ -245,13 +243,15 @@
     wa, wb = jnp.exp(top_a - top), jnp.exp(top_b - top)
     total = (own[:, 1:2] + own[:, 2:3]) * wa + (got[:, 1:2] + got[:, 2:3]) * wb
     usum[...] = usum[...] * wa + us_recv[:, :D].astype(F32) * wb
-    high, low = split2(total)
-    ustat[0:128, :] = lanes((128, 128), (top, high, low))
+    ust[...] = lanes((128, 128), (top, total)).T[0:2, :]
     for j in range(NC):
-        tile = ustat[j * 8 : j * 8 + 8, :]
-        upk[j] = jnp.concatenate(
-            [fold(usum[j * 8 : j * 8 + 8, :]), jnp.concatenate([tile, tile], axis=0)], axis=1
-        ).astype(BF)
+        upk[j] = fold(usum[j * 8 : j * 8 + 8, :]).astype(BF)
+
+    def aw_copy(d):
+        return remote(ust, ustr.at[d], send.at[17], recv.at[16], {"ctx": ahead(d) * 2 + core})
+
+    aw = Copies(open_copies, aw_copy, PLANE, (ustr.at[1:NC], send.at[17]), (ustr.at[1:NC], recv.at[16]))
+    aw.start_all()
 
     def au_copy(d):
         j = ahead(d)
@@ -260,6 +260,7 @@
     au = Copies(open_copies, au_copy, PLANE, (upk.at[0 : NC - 1], send.at[4]), (uarr.at[1:NC], recv.at[4]))
     au.start_all()
     uarr[0] = upk[chip]
+    ustr[0] = ust[...]
 
     gsum[...] = nn(combH[mine, :], g[...])
     sib_g.wait_recv()
@@ -292,13 +293,18 @@
             woT[e, :, at] = wo[e, at, :].T
 
     au.wait_recv()
-    stats = uarr[:, :, half : half + 128].astype(F32)
-    top = jnp.max(stats[:, :, 0:1], axis=0)
-    w = jnp.exp(stats[:, :, 0:1] - top)
-    total = jnp.sum(w * (stats[:, :, 1:2] + stats[:, :, 2:3]), axis=0)
+    aw.wait_recv()
+    utt[...] = jnp.concatenate(
+        [ustr[:, 0, :], ustr[:, 1, :], jnp.zeros((128 - 2 * NC, 128), F32)], axis=0
+    ).T
+    stats = utt[pl.ds(pl.multiple_of(chip * 8, 8), 8), :]
+    stats = jnp.concatenate([stats, stats], axis=0)
+    top = jnp.max(stats[:, :NC], axis=1, keepdims=True)
+    w = jnp.exp(stats[:, :NC] - top)
+    total = jnp.sum(w * stats[:, NC : 2 * NC], axis=1, keepdims=True)
     acc = jnp.zeros((16, half), F32)
     for d in range(NC):
-        acc = acc + w[d] * uarr[d, :, :half].astype(F32)
+        acc = acc + w[:, d : d + 1] * uarr[d].astype(F32)
     acc = acc / total
     rown[...] = acc
     zu[dp] = acc.astype(BF)
@@ -309,7 +315,7 @@
     bu = Copies(open_copies, bu_copy, LINE, (zu.at[0 : NZ - 1], send.at[6]), (zu.at[0 : NZ - 1], recv.at[6]))
     bu.start_all()
     z_high, z_low = split2(total)
-    so[core, chip, :, half:] = lanes((16, 128), (top, z_high, z_low)).astype(BF)
+    sm[core, chip] = lanes((16, 128), (top, z_high, z_low)).astype(BF)
 
     acc = fold(gsum[pl.ds(pl.multiple_of(chip * 8, 8), 8), :])
     ag.wait_recv()
@@ -320,6 +326,20 @@
 
     bg = Copies(open_copies, bg_copy, LINE, (zg.at[0 : NZ - 1], send.at[5]), (zg.at[0 : NZ - 1], recv.at[5]))
     bg.start_all()
+
+    def dm_copy(d):
+        return remote(
+            sm.at[core, chip], sm.at[core, chip], send.at[15], dm_r.at[d], {"ctx": ahead(d) * 2 + core}
+        )
+
+    def fm_copy(d):
+        j = behind(d)
+        return remote(sm.at[core, j], sm.at[core, j], send.at[16], recv.at[15], sib)
+
+    dm = Copies(open_copies, dm_copy, PLANE, (sm.at[0, 0 : NC - 1], send.at[15]))
+    fm = Copies(open_copies, fm_copy, [], (sm.at[0], send.at[16]), (sm.at[0], recv.at[15]))
+    dm.start_all()
+    fm.start(0)
 
     first = lax.rem(lax.broadcasted_iota(jnp.int32, (64, HL), 0), 8) < 4
     bu.wait_recv()
@@ -358,8 +378,12 @@
     cb.start_all()
     b_own = fold(outp[pl.ds(pl.multiple_of(dp * 8, 8), 8), :])
 
+    for d in reversed(PLANE):
+        dm.wait_one(d)
+        fm.start(d)
+
     co.wait_recv()
-    so[core, chip, :, :half] = add_all(o_own, crecv, NZ).astype(BF)
+    so[core, chip] = add_all(o_own, crecv, NZ).astype(BF)
 
     def do_copy(d):
         return remote(
@@ -379,9 +403,21 @@
         for c in range(HL // 128):
             at = slice(c * 128, (c + 1) * 128)
             wogs[e, at, :] = tn(act[e, :, at], gall[...]).astype(BF)
-        for c in range(D // 128):
-            at = slice(c * 128, (c + 1) * 128)
-            wigs[e, at, :] = tn(rall[:, at], pg[e]).astype(BF)
+
+    def stat_of(ref, low):
+        return jnp.concatenate(
+            [ref[k, j, 0:8, low : low + 128].astype(F32) for k in range(2) for j in range(NC)], axis=0
+        )
+
+    fm.wait_recv()
+    stat = stat_of(sm, 0)
+    top = stat[:, 0:1]
+    over = 1.0 / (stat[:, 1:2] + stat[:, 2:3])
+    for t in range(T // 128):
+        at = slice(t * 128, (t + 1) * 128)
+        prob = jnp.exp(LT[:, at] - top) * over
+        LT[:, at] = prob
+        dispH[:, at] = prob.astype(BF)
 
     cb.wait_recv()
     back = add_all(b_own, brecv, NZ).astype(BF)
@@ -405,10 +441,10 @@
     fb = Copies(open_copies, fb_copy, [], (si.at[0], send.at[12]), (si.at[0], recv.at[12]))
     db.start_all()
     fb.start(0)
-
-    for d in reversed(PLANE):
-        do.wait_one(d)
-        fo.start(d)
+    for e in range(2):
+        for c in range(D // 128):
+            at = slice(c * 128, (c + 1) * 128)
+            wigs[e, at, :] = tn(rall[:, at], pg[e]).astype(BF)
 
     def gather(ref, rows, k):
         for q in range(NC // 2):
@@ -416,36 +452,27 @@
                 [unfold(ref[k, 2 * q + i, :, :half].astype(F32)) for i in range(2)], axis=0
             ).astype(BF)
 
-    def stat_of(ref):
-        return jnp.concatenate(
-            [ref[k, j, 0:8, half : half + 128].astype(F32) for k in range(2) for j in range(NC)], axis=0
-        )
-
+    for d in reversed(PLANE):
+        do.wait_one(d)
+        fo.start(d)
     gather(so, sof, core)
     cpart[mine, :] = nt(sof[mine, :], g[...])
+    for d in reversed(PLANE):
+        db.wait_one(d)
+        fb.start(d)
     fo.wait_recv()
     gather(so, sof, other)
     cpart[theirs, :] = nt(sof[theirs, :], g[...])
-    stat = stat_of(so)
-    top = stat[:, 0:1]
-    over = 1.0 / (stat[:, 1:2] + stat[:, 2:3])
     for t in range(T // 128):
         at = slice(t * 128, (t + 1) * 128)
         prob, back = comb[:, at], cpart[:, at]
         cpart[:, at] = prob * (back - jnp.sum(prob * back, axis=0, keepdims=True))
-        prob = jnp.exp(LT[:, at] - top) * over
-        LT[:, at] = prob
-        dispH[:, at] = prob.astype(BF)
-
-    for d in reversed(PLANE):
-        db.wait_one(d)
-        fb.start(d)
     gather(si, sif, core)
     comb[mine, :] = nt(sif[mine, :], x[...])
     fb.wait_recv()
     gather(si, sif, other)
     comb[theirs, :] = nt(sif[theirs, :], x[...])
-    stat = stat_of(si)
+    stat = stat_of(si, half)
     inner = stat[:, 0:1] + stat[:, 1:2]
     for t in range(T // 128):
         at = slice(t * 128, (t + 1) * 128)
@@ -528,19 +555,21 @@
             vmem((128, D), BF), vmem((128, D), BF), vmem((128, D), F32),
             vmem((NC, 16, half), BF), vmem((NC, 16, half), BF),
             vmem((128, D + 128), BF), vmem((128, D + 128), BF), vmem((128, D), F32), vmem((S, 128), F32),
-            vmem((NC, 16, half + 128), BF), vmem((NC, 16, half + 128), BF),
+            vmem((NC, 16, half), BF), vmem((NC, 16, half), BF),
+            vmem((2, 128), F32), vmem((NC, 2, 128), F32), vmem((128, 128), F32),
             vmem((2, HL, D), BF), vmem((2, D, HL), BF),
             vmem((16, half), F32), vmem((NZ, 16, half), BF), vmem((NZ, 16, half), BF),
             vmem((64, D), BF), vmem((64, D), BF), vmem((64, HL), F32),
             vmem((2, 64, HL), BF), vmem((2, 64, HL), BF), vmem((64, D), F32),
             vmem((NZ, 16, half), BF), vmem((NZ, 16, half), BF),
             vmem((NZ, 16, half), BF), vmem((NZ, 16, half), BF),
-            vmem((2, NC, 16, half + 128), BF), vmem((2, NC, 16, half + 128), BF), vmem((S, D), BF), vmem((S, D), BF),
+            vmem((2, NC, 16, half), BF), vmem((2, NC, 16, half + 128), BF), vmem((2, NC, 16, 128), BF),
+            vmem((S, D), BF), vmem((S, D), BF),
             vmem((S, T), F32), vmem((S, T), BF), vmem((S, T), BF), vmem((S, T), BF),
             vmem((D // 2, S), BF), vmem((D // 2, S), BF), vmem((D // 2, S), F32),
             vmem((NC, 32, S), BF), vmem((NC, 32, S), BF), vmem((32, S), BF), vmem((NZ, 32, S), BF),
-            pltpu.SemaphoreType.DMA((8,)), pltpu.SemaphoreType.DMA((15,)), pltpu.SemaphoreType.DMA((15,)),
-            pltpu.SemaphoreType.DMA((NC,)), pltpu.SemaphoreType.DMA((NC,)),
+            pltpu.SemaphoreType.DMA((5,)), pltpu.SemaphoreType.DMA((18,)), pltpu.SemaphoreType.DMA((17,)),
+            pltpu.SemaphoreType.DMA((NC,)), pltpu.SemaphoreType.DMA((NC,)), pltpu.SemaphoreType.DMA((NC,)),
         ],
         compiler_params=pltpu.CompilerParams(
             collective_id=0, has_side_effects=True, vmem_limit_bytes=36 * 2**20

time: 58.7 us -> 56.3 us (0.959)
  Pallas kernels: 57.4 us -> 55.1 us
    pallas_call x1, Pallas kernels: 54.9 us -> 52.6 us  [per_device(): pl.pallas_call(kernel, out_shape=(pltpu.VMEM((T, D), BF), pltpu.VMEM((32,...]
where the time goes in v4:
time: 56.3 us; the launch traced here: 55.7 us
  Pallas kernels  55.1 us (98%)
  between operations  0.64 us (1%)
    pallas_call x1, Pallas kernels, per_device(): pl.pallas_call(kernel, out_shape=(pltpu.VMEM((T, D), BF), pltpu.VMEM((32,...  52.6 us
    pallas_call x1, Pallas kernels, per_device(): pl.pallas_call(store_kernel, out_shape=(pltpu.HBM((T, D), BF), pltpu.HBM(...  2.48 us

profile of v4, /device:TPU:2, one launch (start us, length us, event | category | flops | bytes accessed | tf_op | source)
XLA Modules:
  0.0 55.7 jit_solution(11693558684331532893)
XLA Ops:
  0.6 52.6 %shard_map.84 = (bf16[640,1024]{1,0:T(8,128)(2,1)S(1)}, f32[32,256]{1,0:T(8,128)S(1)}, bf16[2,1024,512]{2,1,0:T(8,128)(2,1)S(1)}, bf16[2,512,1024]{2,1,0:T(8,128)(2,1)S(1)}) custom-call(bf16[640,1024]{1,0:T(8,128)(2,1)} %bitcast.3, bf16[1024,256]{1,0:T(8,128)(2,1)} %keys_hbm.1, bf16[2,1024,512]{2,1,0:T(8,128)(2,1)} %wi_hbm.1, bf16[2,512,1024]{2,1,0:T(8,128)(2,1)} %wo_hbm.1, ...), custom_call_target="tpu_custom_call" | custom-call | flops 4000000000 | bytes 13000000 | tf_op jit(solution)/shard_map/pallas_call | solution.py:541
  53.2 2.5 %shard_map.85 = (bf16[640,1024]{1,0:T(8,128)(2,1)}, f32[32,256]{1,0:T(8,128)}, bf16[2,1024,512]{2,1,0:T(8,128)(2,1)}, bf16[2,512,1024]{2,1,0:T(8,128)(2,1)}) custom-call(bf16[640,1024]{1,0:T(8,128)(2,1)S(1)} %get-tuple-element.12.tgs, f32[32,256]{1,0:T(8,128)S(1)} %get-tuple-element.13.kout, bf16[2,1024,512]{2,1,0:T(8,128)(2,1)S(1)} %get-tuple-element.14.wigs, ...), custom_call_target="tpu_custom_call" | custom-call | tf_op jit(solution)/shard_map/pallas_call | solution.py:579

commit v5 on v4

--- a/solution.py
+++ b/solution.py
@@ -457,9 +457,6 @@
         fo.start(d)
     gather(so, sof, core)
     cpart[mine, :] = nt(sof[mine, :], g[...])
-    for d in reversed(PLANE):
-        db.wait_one(d)
-        fb.start(d)
     fo.wait_recv()
     gather(so, sof, other)
     cpart[theirs, :] = nt(sof[theirs, :], g[...])
@@ -467,6 +464,9 @@
         at = slice(t * 128, (t + 1) * 128)
         prob, back = comb[:, at], cpart[:, at]
         cpart[:, at] = prob * (back - jnp.sum(prob * back, axis=0, keepdims=True))
+    for d in reversed(PLANE):
+        db.wait_one(d)
+        fb.start(d)
     gather(si, sif, core)
     comb[mine, :] = nt(sif[mine, :], x[...])
     fb.wait_recv()

time: 56.3 us -> 55.8 us (level)
  no operation moved by 1% of the time
where the time goes in v5:
time: 55.8 us; the launch traced here: 55.7 us
  Pallas kernels  55 us (99%)
  between operations  0.64 us (1%)
    pallas_call x1, Pallas kernels, per_device(): pl.pallas_call(kernel, out_shape=(pltpu.VMEM((T, D), BF), pltpu.VMEM((32,...  52.6 us
    pallas_call x1, Pallas kernels, per_device(): pl.pallas_call(store_kernel, out_shape=(pltpu.HBM((T, D), BF), pltpu.HBM(...  2.48 us

profile of v5, /device:TPU:2, one launch (start us, length us, event | category | flops | bytes accessed | tf_op | source)
XLA Modules:
  0.0 55.7 jit_solution(12804365058580187271)
XLA Ops:
  0.6 52.6 %shard_map.84 = (bf16[640,1024]{1,0:T(8,128)(2,1)S(1)}, f32[32,256]{1,0:T(8,128)S(1)}, bf16[2,1024,512]{2,1,0:T(8,128)(2,1)S(1)}, bf16[2,512,1024]{2,1,0:T(8,128)(2,1)S(1)}) custom-call(bf16[640,1024]{1,0:T(8,128)(2,1)} %bitcast.3, bf16[1024,256]{1,0:T(8,128)(2,1)} %keys_hbm.1, bf16[2,1024,512]{2,1,0:T(8,128)(2,1)} %wi_hbm.1, bf16[2,512,1024]{2,1,0:T(8,128)(2,1)} %wo_hbm.1, ...), custom_call_target="tpu_custom_call" | custom-call | flops 4000000000 | bytes 13000000 | tf_op jit(solution)/shard_map/pallas_call | solution.py:541
  53.2 2.5 %shard_map.85 = (bf16[640,1024]{1,0:T(8,128)(2,1)}, f32[32,256]{1,0:T(8,128)}, bf16[2,1024,512]{2,1,0:T(8,128)(2,1)}, bf16[2,512,1024]{2,1,0:T(8,128)(2,1)}) custom-call(bf16[640,1024]{1,0:T(8,128)(2,1)S(1)} %get-tuple-element.12.tgs, f32[32,256]{1,0:T(8,128)S(1)} %get-tuple-element.13.kout, bf16[2,1024,512]{2,1,0:T(8,128)(2,1)S(1)} %get-tuple-element.14.wigs, ...), custom_call_target="tpu_custom_call" | custom-call | tf_op jit(solution)/shard_map/pallas_call | solution.py:579

commit v6 on v5

--- a/solution.py
+++ b/solution.py
@@ -105,6 +105,7 @@
             else:
                 self.wait_recv()
         if self.to_send:
+            self.to_send = False
             ref, sem = self.sent
             pltpu.make_async_copy(ref, ref, sem).wait()
 
@@ -506,6 +507,9 @@
         at = slice(t * 128, (t + 1) * 128)
         tgs[at, :] = (tn(lgH[:, at], keysT[...]) + tn(dispH[:, at], sif[...])).astype(BF)
 
+    for copies in open_copies:
+        if copies is not fk:
+            copies.drain()
     fk.wait_recv()
     acc = add_all(ksum[pl.ds(pl.multiple_of(chip * 32, 32), 32), :], karr, NC)
     kz[...] = acc.astype(BF)
@@ -518,6 +522,7 @@
 
     fz.start_all()
 
+    fk.drain()
     fz.wait_recv()
     kout[...] = add_all(acc, kzarr, NZ)
 

time: 55.8 us -> 55.8 us (level)
  no operation moved by 1% of the time
where the time goes in v6:
time: 55.8 us; the launch traced here: 55.6 us
  Pallas kernels  55 us (99%)
  between operations  0.64 us (1%)
    pallas_call x1, Pallas kernels, per_device(): pl.pallas_call(kernel, out_shape=(pltpu.VMEM((T, D), BF), pltpu.VMEM((32,...  52.5 us
    pallas_call x1, Pallas kernels, per_device(): pl.pallas_call(store_kernel, out_shape=(pltpu.HBM((T, D), BF), pltpu.HBM(...  2.48 us

profile of v6, /device:TPU:2, one launch (start us, length us, event | category | flops | bytes accessed | tf_op | source)
XLA Modules:
  0.0 55.6 jit_solution(9518386931356994049)
XLA Ops:
  0.6 52.5 %shard_map.84 = (bf16[640,1024]{1,0:T(8,128)(2,1)S(1)}, f32[32,256]{1,0:T(8,128)S(1)}, bf16[2,1024,512]{2,1,0:T(8,128)(2,1)S(1)}, bf16[2,512,1024]{2,1,0:T(8,128)(2,1)S(1)}) custom-call(bf16[640,1024]{1,0:T(8,128)(2,1)} %bitcast.3, bf16[1024,256]{1,0:T(8,128)(2,1)} %keys_hbm.1, bf16[2,1024,512]{2,1,0:T(8,128)(2,1)} %wi_hbm.1, bf16[2,512,1024]{2,1,0:T(8,128)(2,1)} %wo_hbm.1, ...), custom_call_target="tpu_custom_call" | custom-call | flops 4000000000 | bytes 13000000 | tf_op jit(solution)/shard_map/pallas_call | solution.py:546
  53.2 2.5 %shard_map.85 = (bf16[640,1024]{1,0:T(8,128)(2,1)}, f32[32,256]{1,0:T(8,128)}, bf16[2,1024,512]{2,1,0:T(8,128)(2,1)}, bf16[2,512,1024]{2,1,0:T(8,128)(2,1)}) custom-call(bf16[640,1024]{1,0:T(8,128)(2,1)S(1)} %get-tuple-element.12.tgs, f32[32,256]{1,0:T(8,128)S(1)} %get-tuple-element.13.kout, bf16[2,1024,512]{2,1,0:T(8,128)(2,1)S(1)} %get-tuple-element.14.wigs, ...), custom_call_target="tpu_custom_call" | custom-call | tf_op jit(solution)/shard_map/pallas_call | solution.py:584
